TPU v7x, 512 devices: a whole 4x4x16 slice. The times are simulated.
512 devices in a mesh: dom: 128 (over z, y, core), slab: 4 (over x).
Axes of the slice: x: 4, y: 4, z: 16, core: 2. Of those that a mesh axis runs over, the one named last changes fastest.
Arguments:
- features: bfloat16 [65536, 128], P(('dom', 'slab')), may hold values from -6 to 6
- positions: float32 [3, 65536], P(None, ('dom', 'slab')), may hold values from 0 to 4
- neighbours: int32 [32, 65536], P(None, ('dom', 'slab')), may hold values from 0 to 415, as said below
- neighbour_mask: int32 [32, 65536], P(None, ('dom', 'slab')), may hold values from 0 to 1
- ghost_list: int32 [16384], P(('dom', 'slab')), may hold values from 0 to 127, as said below
- w_up: bfloat16 [128, 128], replicated, may hold values from -0.5 to 0.5
- radial_weight_1: bfloat16 [8, 64], replicated, may hold values from -2 to 2
- radial_weight_2: bfloat16 [64, 64], replicated, may hold values from -0.75 to 0.75
- radial_weight_3: bfloat16 [64, 256], replicated, may hold values from -0.75 to 0.75
- w_a: bfloat16 [128, 128], replicated, may hold values from -0.5 to 0.5
- w_b: bfloat16 [128, 128], replicated, may hold values from -0.5 to 0.5
- w_o1: bfloat16 [128, 16], replicated, may hold values from -0.5 to 0.5
- w_o2: float32 [16], replicated, may hold values from -1.5 to 1.5
Outputs:
- energies: float32 [65536], P(('dom', 'slab'))
- forces: float32 [3, 65536], P(None, ('dom', 'slab'))
Inputs may be any that keep to these rules, and one draw needn't show every extreme that they name: `neighbours`: A value below 128 is a local atom other than the slot's own atom; a larger value is 128 + b * 32 + r with block b in 0 .. 8 but never 4. `ghost_list`: the 32 entries of each domain are distinct.
All inputs are finite; a program needn't handle non-finite values.
Results may differ from a plain program's by a relative error of at most 0.015.
Values may be sent and summed in bfloat16 or wider, within the bound.
A program may use at most 64 MiB of HBM per device.

v0:
```python
import jax
import jax.numpy as jnp
from jax import lax
from jax.sharding import PartitionSpec as P

pairwise_scale = 1.0 / 16.0
cell_width = 4.0
exact = lax.Precision.HIGHEST


def from_behind(value, axis, steps):
    count = lax.axis_size(axis)
    pairs = [(source, (source + steps) % count) for source in range(count)]
    return lax.ppermute(value, axis, pairs)


def extended(x, sides, width):
    for axis, dim in sides:
        peers, length = (lax.axis_size(axis), x.shape[dim])
        up = [(i, (i + 1) % peers) for i in range(peers)]
        down = [(j, i) for i, j in up]
        last = lax.slice_in_dim(x, length - width, length, axis=dim)
        first = lax.slice_in_dim(x, 0, width, axis=dim)
        before = lax.ppermute(last, axis, up)
        after = lax.ppermute(first, axis, down)
        x = jnp.concatenate([before, x, after], axis=dim)
    return x


def pair_messages(
    atom_coords,
    neighbour_coords,
    atom_projection,
    neighbour_projection,
    alive_flags,
    radial_weight_1,
    radial_weight_2,
    radial_weight_3,
):
    offset = neighbour_coords - atom_coords
    spread = jnp.sqrt(jnp.sum(offset * offset, axis=0) + 1.0)
    centers = 1.0 + 0.75 * jnp.arange(radial_weight_1.shape[0], dtype=jnp.float32)
    basis = jnp.exp(-jnp.square(spread[:, None] - centers[None, :])).astype(jnp.bfloat16)
    layer_one = jax.nn.silu(
        jnp.dot(basis, radial_weight_1, preferred_element_type=jnp.float32)
    ).astype(jnp.bfloat16)
    second_layer = jax.nn.silu(
        jnp.dot(layer_one, radial_weight_2, preferred_element_type=jnp.float32)
    ).astype(jnp.bfloat16)
    radial_filter = (
        jnp.dot(second_layer, radial_weight_3, preferred_element_type=jnp.float32)
        * (alive_flags * pairwise_scale)[:, None]
    )
    channels = atom_projection.shape[1]
    scalar_weight = radial_filter[:, :channels]
    vector_weight = radial_filter[:, channels:]
    direction = offset / spread[None, :]
    partner_wide = neighbour_projection.astype(jnp.float32)
    atom_wide = atom_projection.astype(jnp.float32)
    atom_scalar_message = scalar_weight * partner_wide
    atom_vector_message = direction[:, :, None] * (vector_weight * partner_wide)[None]
    neighbour_scalar_message = scalar_weight * atom_wide
    neighbour_vector_message = -direction[:, :, None] * (vector_weight * atom_wide)[None]
    return (
        atom_scalar_message,
        atom_vector_message,
        neighbour_scalar_message,
        neighbour_vector_message,
    )


def node_energy(agg_s, agg_v, features, w_a, w_b, w_o1, w_o2):
    norms = jnp.sum(agg_v * agg_v, axis=0)
    mixed = features.astype(jnp.float32) + jnp.dot(
        agg_s.astype(jnp.bfloat16), w_a, preferred_element_type=jnp.float32
    )
    mixed = mixed + jnp.dot(norms.astype(jnp.bfloat16), w_b, preferred_element_type=jnp.float32)
    hidden = jax.nn.silu(
        jnp.dot(mixed.astype(jnp.bfloat16), w_o1, preferred_element_type=jnp.float32)
    )
    return jnp.sum(hidden * w_o2[None, :], axis=1)


def return_sums(packed):
    result = packed[1, 1]
    for across in (-1, 0, 1):
        for along in (-1, 0, 1):
            if across != 0 or along != 0:
                moving = packed[1 + across, 1 + along]
                if across != 0:
                    moving = from_behind(moving, "dom", across)
                if along != 0:
                    moving = from_behind(moving, "slab", along)
                result = result + moving
    return result


def add_rows(target, piece, start_offset, dim):
    current = lax.dynamic_slice_in_dim(target, start_offset, piece.shape[dim], dim)
    return lax.dynamic_update_slice_in_dim(target, current + piece, start_offset, dim)


def body(
    features,
    positions,
    neighbours,
    neighbour_mask,
    ghost_list,
    w_up,
    radial_weight_1,
    radial_weight_2,
    radial_weight_3,
    w_a,
    w_b,
    w_o1,
    w_o2,
):
    atoms = features.shape[0]
    channels = features.shape[1]
    boundary = ghost_list.shape[0]
    slots = neighbours.shape[0]
    ext_rows = atoms + 9 * boundary
    proj = jnp.dot(features, w_up, preferred_element_type=jnp.float32).astype(jnp.bfloat16)
    sent_proj = proj[ghost_list].reshape(1, 1, boundary, channels)
    ghost_proj = extended(sent_proj, (("dom", 0), ("slab", 1)), 1)
    sent_pos = positions[:, ghost_list].reshape(1, 1, 3, boundary)
    ghost_pos = extended(sent_pos, (("dom", 0), ("slab", 1)), 1)
    ghost_pos = jnp.transpose(ghost_pos, (2, 0, 1, 3))
    extended_projection = jnp.concatenate(
        [proj, ghost_proj.reshape(9 * boundary, channels)], axis=0
    )
    lanes = (jnp.arange(3, dtype=jnp.float32) - 1.0) * cell_width
    offsets = jnp.stack(
        [
            jnp.broadcast_to(lanes[:, None], (3, 3)),
            jnp.broadcast_to(lanes[None, :], (3, 3)),
            jnp.zeros((3, 3), jnp.float32),
        ]
    )
    ghost_pos = (ghost_pos + offsets[:, :, :, None]).reshape(3, 9 * boundary)
    extended_coords = jnp.concatenate([positions, ghost_pos], axis=1)
    alive_flags_full = (neighbour_mask != 0).astype(jnp.float32)
    rows_of_width = 64
    rounds = atoms // rows_of_width
    row_numbers = jnp.arange(ext_rows, dtype=jnp.int32)

    def edge_tile(slot_index):
        start_offset = (slot_index * rows_of_width).astype(jnp.int32)
        neighbour_table = lax.dynamic_slice_in_dim(
            neighbours, start_offset, rows_of_width, 1
        ).reshape(-1)
        alive_flags = lax.dynamic_slice_in_dim(
            alive_flags_full, start_offset, rows_of_width, 1
        ).reshape(-1)
        owned_coords = lax.dynamic_slice_in_dim(positions, start_offset, rows_of_width, 1)
        owned_coords = jnp.broadcast_to(
            owned_coords[:, None, :], (3, slots, rows_of_width)
        ).reshape(3, -1)
        owned_projection = lax.dynamic_slice_in_dim(proj, start_offset, rows_of_width, 0)
        owned_projection = jnp.broadcast_to(
            owned_projection[None], (slots, rows_of_width, channels)
        ).reshape(-1, channels)
        selector = neighbour_table[:, None] == row_numbers[None, :]
        selector_wide = selector.astype(jnp.float32)
        partner_projection = jnp.dot(
            selector.astype(jnp.bfloat16), extended_projection, preferred_element_type=jnp.float32
        ).astype(jnp.bfloat16)
        partner_coords = jnp.einsum("ce,ne->cn", extended_coords, selector_wide, precision=exact)
        return (
            start_offset,
            selector_wide,
            alive_flags,
            owned_coords,
            owned_projection,
            partner_projection,
            partner_coords,
        )

    def forward_round(slot_index, carry):
        agg_s, agg_v = carry
        (
            start_offset,
            selector_wide,
            alive_flags,
            owned_coords,
            owned_projection,
            partner_projection,
            partner_coords,
        ) = edge_tile(slot_index)
        (
            atom_scalar_message,
            atom_vector_message,
            neighbour_scalar_message,
            neighbour_vector_message,
        ) = pair_messages(
            owned_coords,
            partner_coords,
            owned_projection,
            partner_projection,
            alive_flags,
            radial_weight_1,
            radial_weight_2,
            radial_weight_3,
        )
        own_s = jnp.sum(atom_scalar_message.reshape(slots, rows_of_width, channels), axis=0)
        own_v = jnp.sum(atom_vector_message.reshape(3, slots, rows_of_width, channels), axis=1)
        agg_s = add_rows(agg_s, own_s, start_offset, 0) + jnp.einsum(
            "ne,nc->ec", selector_wide, neighbour_scalar_message, precision=exact
        )
        agg_v = add_rows(agg_v, own_v, start_offset, 1) + jnp.einsum(
            "ne,knc->kec", selector_wide, neighbour_vector_message, precision=exact
        )
        return (agg_s, agg_v)

    start_s = jnp.zeros((ext_rows, channels), jnp.float32)
    start_v = jnp.zeros((3, ext_rows, channels), jnp.float32)
    agg_s, agg_v = lax.fori_loop(0, rounds, forward_round, (start_s, start_v))
    ghost_s = agg_s[atoms:].reshape(3, 3, 1, boundary, channels)
    ghost_v = jnp.moveaxis(agg_v[:, atoms:].reshape(3, 3, 3, boundary, channels), 0, 2)
    returned = return_sums(jnp.concatenate([ghost_s, ghost_v], axis=2))
    local_s = agg_s[:atoms].at[ghost_list].add(returned[0])
    local_v = agg_v[:, :atoms].at[:, ghost_list].add(returned[1:])

    def energy_of(summed, vectors):
        return node_energy(summed, vectors, features, w_a, w_b, w_o1, w_o2)

    energies, pull_nodes = jax.vjp(energy_of, local_s, local_v)
    cot_s, cot_v = pull_nodes(jnp.ones_like(energies))
    sent_cot = jnp.concatenate([cot_s[ghost_list][None], cot_v[:, ghost_list]], axis=0)
    ghost_cot = extended(
        sent_cot.reshape(1, 1, 4, boundary, channels), (("dom", 0), ("slab", 1)), 1
    )
    ext_cot_s = jnp.concatenate([cot_s, ghost_cot[:, :, 0].reshape(9 * boundary, channels)], axis=0)
    ext_cot_v = jnp.concatenate(
        [cot_v, jnp.moveaxis(ghost_cot[:, :, 1:], 2, 0).reshape(3, 9 * boundary, channels)], axis=1
    )

    def backward_round(slot_index, grad):
        (
            start_offset,
            selector_wide,
            alive_flags,
            owned_coords,
            owned_projection,
            partner_projection,
            partner_coords,
        ) = edge_tile(slot_index)

        def positional(atom_endpoint, neighbour_endpoint):
            return pair_messages(
                atom_endpoint,
                neighbour_endpoint,
                owned_projection,
                partner_projection,
                alive_flags,
                radial_weight_1,
                radial_weight_2,
                radial_weight_3,
            )

        ignored, pull_edges = jax.vjp(positional, owned_coords, partner_coords)
        own_cot_s = lax.dynamic_slice_in_dim(cot_s, start_offset, rows_of_width, 0)
        own_cot_s = jnp.broadcast_to(own_cot_s[None], (slots, rows_of_width, channels)).reshape(
            -1, channels
        )
        own_cot_v = lax.dynamic_slice_in_dim(cot_v, start_offset, rows_of_width, 1)
        own_cot_v = jnp.broadcast_to(
            own_cot_v[:, None], (3, slots, rows_of_width, channels)
        ).reshape(3, -1, channels)
        partner_cot_s = jnp.einsum("ne,ec->nc", selector_wide, ext_cot_s, precision=exact)
        partner_cot_v = jnp.einsum("ne,kec->knc", selector_wide, ext_cot_v, precision=exact)
        atom_grad, partner_grad = pull_edges((own_cot_s, own_cot_v, partner_cot_s, partner_cot_v))
        own_grad = jnp.sum(atom_grad.reshape(3, slots, rows_of_width), axis=1)
        return add_rows(grad, own_grad, start_offset, 1) + jnp.einsum(
            "kn,ne->ke", partner_grad, selector_wide, precision=exact
        )

    grad = lax.fori_loop(0, rounds, backward_round, jnp.zeros((3, ext_rows), jnp.float32))
    ghost_grad = jnp.moveaxis(grad[:, atoms:].reshape(3, 3, 3, boundary), 0, 2)
    returned_grad = return_sums(ghost_grad)
    local_grad = grad[:, :atoms].at[:, ghost_list].add(returned_grad)
    return (energies, -local_grad)


def solution(mesh):
    in_specs = (
        P(("dom", "slab"), None),
        P(None, ("dom", "slab")),
        P(None, ("dom", "slab")),
        P(None, ("dom", "slab")),
        P(("dom", "slab")),
        P(),
        P(),
        P(),
        P(),
        P(),
        P(),
        P(),
        P(),
    )
    out_specs = (P(("dom", "slab")), P(None, ("dom", "slab")))
    return jax.shard_map(body, mesh=mesh, in_specs=in_specs, out_specs=out_specs, check_vma=False)
```

profile of v0, /device:TPU:6, one launch (start us, length us, event | category | flops | bytes accessed | tf_op | source)
XLA Modules:
  0.0 279.8 jit_solution(7473065262397402486)
XLA Ops:
  3.3 13.3 %collective-permute-start.1 = (f32[1,1,3,32]{3,2,1,0:T(4,128)S(1)}, f32[1,1,3,32]{3,2,1,0:T(4,128)S(1)}, u32[]{:S(2)}, u32[]{:S(2)}) collective-permute-start(f32[1,1,3,32]{3,2,1,0:T(4,128)S(1)} %bitcast.261), channel_id=1, source_target_pairs={{4,0},{8,4},{12,8},{16,12},{20,16},{24,20},{28,24},{32,28},{36,32}... | collective-permute-start | bytes 1160 | tf_op jit(solution)/shard_map/ppermute | solution.py:25
  21.3 7.0 %collective-permute-start.5 = (bf16[1,1,32,128]{3,2,1,0:T(8,128)(2,1)S(1)}, bf16[1,1,32,128]{3,2,1,0:T(8,128)(2,1)S(1)}, u32[]{:S(2)}, u32[]{:S(2)}) collective-permute-start(bf16[1,1,32,128]{3,2,1,0:T(8,128)(2,1)S(1)} %bitcast.253), channel_id=1, source_target_pairs={{4,0},{8,4},{12,8},{16,12},{20,16},{24,20},{28,24},{32,28},{36,32}... | collective-permute-start | bytes 24584 | tf_op jit(solution)/shard_map/ppermute | solution.py:25
  31.3 2.7 collective-permute-start.3
  34.0 4.3 %collective-permute-start.2 = (f32[3,1,3,32]{3,2,1,0:T(4,128)S(1)}, f32[3,1,3,32]{3,2,1,0:T(4,128)S(1)}, u32[]{:S(2)}, u32[]{:S(2)}) collective-permute-start(f32[3,1,3,32]{3,2,1,0:T(4,128)S(1)} %pad_maximum_fusion.9), channel_id=1, source_target_pairs={{0,1},{1,2},{2,3},{3,0},{4,5},{5,6},{6,7},{7,4},{8,9},{9,10},{10,1... | collective-permute-start | bytes 3464 | tf_op jit(solution)/shard_map/ppermute | solution.py:24
  42.2 5.0 %collective-permute-start.6 = (bf16[3,1,32,128]{3,2,1,0:T(8,128)(2,1)S(1)}, bf16[3,1,32,128]{3,2,1,0:T(8,128)(2,1)S(1)}, u32[]{:S(2)}, u32[]{:S(2)}) collective-permute-start(bf16[3,1,32,128]{3,2,1,0:T(8,128)(2,1)S(1)} %pad_maximum_fusion.8), channel_id=1, source_target_pairs={{0,1},{1,2},{2,3},{3,0},{4,5},{5,6},{6,7},{7,4},{8,9},{9,10},{10,1... | collective-permute-start | bytes 73736 | tf_op jit(solution)/shard_map/ppermute | solution.py:24
  49.5 41.8 %while.30 = (s32[]{:T(128)}, f32[416,128]{1,0:T(8,128)S(1)}, f32[3,416,128]{2,1,0:T(8,128)S(1)}, s32[32,128]{1,0:T(8,128)}, f32[3,416]{1,0:T(4,128)}, /*index=5*...) while((s32[]{:T(128)}, f32[416,128]{1,0:T(8,128)S(1)}, ...), condition=%wide.region_4.5_spmd.clone, body=%wide.region_0.4_spmd.clone.sunk | while | flops 5579218944 | bytes 22766100 | solution.py:217
  59.9 3.8 %fusion.238 = f32[416,128]{1,0:T(8,128)} fusion(f32[416,128]{1,0:T(8,128)S(1)} %add_dynamic-update-slice_fusion.4, f32[2048,128]{1,0:T(8,128)} %get-tuple-element.930, s32[2048]{0:T(1024)S(1)} %eq.217), kind=kOutput, calls=%fused_computation.32.clone.1 | convolution fusion | flops 1309528064 | bytes 1482752 | tf_op jit(solution)/shard_map/while/body/eval_jaxpr/ne,nc->ec/dot_general | solution.py:207
  66.2 4.2 %fusion.240 = f32[3,416,128]{2,1,0:T(8,128)S(1)} fusion(f32[3,416,128]{2,1,0:T(8,128)S(1)} %add_dynamic-update-slice_fusion.5, s32[2048]{0:T(1024)S(1)} %eq.217, f32[2048,128]{1,0:T(8,128)S(1)} %copy-done.2, f32[3,2048]{1,0:T(4,128)} %get-tuple-element.935), kind=kOutput, calls=%fused_computation.31.clone.1 | convolution fusion | flops 3927666688 | bytes 2359296 | tf_op jit(solution)/shard_map/while/body/eval_jaxpr/ne,knc->kec/dot_general | solution.py:210
  80.8 3.8 %fusion.238 = f32[416,128]{1,0:T(8,128)} fusion(f32[416,128]{1,0:T(8,128)S(1)} %add_dynamic-update-slice_fusion.4, f32[2048,128]{1,0:T(8,128)} %get-tuple-element.930, s32[2048]{0:T(1024)S(1)} %eq.217), kind=kOutput, calls=%fused_computation.32.clone.1 | convolution fusion | flops 1309528064 | bytes 1482752 | tf_op jit(solution)/shard_map/while/body/eval_jaxpr/ne,nc->ec/dot_general | solution.py:207
  87.1 4.2 %fusion.240 = f32[3,416,128]{2,1,0:T(8,128)S(1)} fusion(f32[3,416,128]{2,1,0:T(8,128)S(1)} %add_dynamic-update-slice_fusion.5, s32[2048]{0:T(1024)S(1)} %eq.217, f32[2048,128]{1,0:T(8,128)S(1)} %copy-done.2, f32[3,2048]{1,0:T(4,128)} %get-tuple-element.935), kind=kOutput, calls=%fused_computation.31.clone.1 | convolution fusion | flops 3927666688 | bytes 2359296 | tf_op jit(solution)/shard_map/while/body/eval_jaxpr/ne,knc->kec/dot_general | solution.py:210
  97.2 5.4 %collective-permute-start.14 = (f32[4,32,128]{2,1,0:T(8,128)S(1)}, f32[4,32,128]{2,1,0:T(8,128)S(1)}, u32[]{:S(2)}, u32[]{:S(2)}) collective-permute-start(f32[4,32,128]{2,1,0:T(8,128)S(1)} %get-tuple-element.740), channel_id=1, source_target_pairs={{0,1},{1,2},{2,3},{3,0},{4,5},{5,6},{6,7},{7,4},{8,9},{9,10},{10,1... | collective-permute-start | bytes 196616 | tf_op jit(solution)/shard_map/ppermute | solution.py:14
  104.6 6.7 %collective-permute-start.11 = (f32[4,32,128]{2,1,0:T(8,128)S(1)}, f32[4,32,128]{2,1,0:T(8,128)S(1)}, u32[]{:S(2)}, u32[]{:S(2)}) collective-permute-start(f32[4,32,128]{2,1,0:T(8,128)S(1)} %get-tuple-element.738), channel_id=1, source_target_pairs={{0,508},{4,0},{8,4},{12,8},{16,12},{20,16},{24,20},{28,24},{32,28}... | collective-permute-start | bytes 196616 | tf_op jit(solution)/shard_map/ppermute | solution.py:14
  111.3 2.7 collective-permute-start.8
  114.0 3.4 %collective-permute-start.10 = (f32[4,32,128]{2,1,0:T(8,128)S(1)}, f32[4,32,128]{2,1,0:T(8,128)S(1)}, u32[]{:S(2)}, u32[]{:S(2)}) collective-permute-start(f32[4,32,128]{2,1,0:T(8,128)S(1)} %get-tuple-element.737), channel_id=1, source_target_pairs={{0,508},{4,0},{8,4},{12,8},{16,12},{20,16},{24,20},{28,24},{32,28}... | collective-permute-start | bytes 196616 | tf_op jit(solution)/shard_map/ppermute | solution.py:14
  117.4 4.9 %collective-permute-start.19 = (f32[4,32,128]{2,1,0:T(8,128)S(1)}, f32[4,32,128]{2,1,0:T(8,128)S(1)}, u32[]{:S(2)}, u32[]{:S(2)}) collective-permute-start(f32[4,32,128]{2,1,0:T(8,128)S(1)} %collective-permute-done.18), channel_id=1, source_target_pairs={{0,1},{1,2},{2,3},{3,0},{4,5},{5,6},{6,7},{7,4},{8,9},{9,10},{10,1... | collective-permute-start | bytes 196616 | tf_op jit(solution)/shard_map/ppermute | solution.py:14
  124.2 5.1 %collective-permute-start.12 = (f32[4,32,128]{2,1,0:T(8,128)S(1)}, f32[4,32,128]{2,1,0:T(8,128)S(1)}, u32[]{:S(2)}, u32[]{:S(2)}) collective-permute-start(f32[4,32,128]{2,1,0:T(8,128)S(1)} %collective-permute-done.11), channel_id=1, source_target_pairs={{0,1},{1,2},{2,3},{3,0},{4,5},{5,6},{6,7},{7,4},{8,9},{9,10},{10,1... | collective-permute-start | bytes 196616 | tf_op jit(solution)/shard_map/ppermute | solution.py:14
  131.9 4.8 %collective-permute-done.9 = f32[4,32,128]{2,1,0:T(8,128)S(1)} collective-permute-done((f32[4,32,128]{2,1,0:T(8,128)S(1)}, f32[4,32,128]{2,1,0:T(8,128)S(1)}, u32[]{:S(2)}, u32[]{:S(2)}) %collective-permute-start.9) | collective-permute-done | bytes 65568 | tf_op jit(solution)/shard_map/ppermute | solution.py:14
  148.4 6.5 %collective-permute-done.20 = f32[1,1,4,32,128]{4,2,3,1,0:T(4,128)S(1)} collective-permute-done((f32[1,1,4,32,128]{4,2,3,1,0:T(4,128)S(1)}, f32[1,1,4,32,128]{4,2,3,1,0:T(4,128)S(1)}, u32[]{:S(2)}, u32[]{:S(2)}) %collective-permute-start.20) | collective-permute-done | bytes 65568 | tf_op jit(solution)/shard_map/ppermute | solution.py:24
  156.9 5.1 %collective-permute-start.22 = (f32[3,1,4,32,128]{4,2,3,1,0:T(4,128)S(1)}, f32[3,1,4,32,128]{4,2,3,1,0:T(4,128)S(1)}, u32[]{:S(2)}, u32[]{:S(2)}) collective-permute-start(f32[3,1,4,32,128]{4,2,3,1,0:T(4,128)S(1)} %pad_maximum_fusion.3), channel_id=1, source_target_pairs={{0,1},{1,2},{2,3},{3,0},{4,5},{5,6},{6,7},{7,4},{8,9},{9,10},{10,1... | collective-permute-start | bytes 589832 | tf_op jit(solution)/shard_map/ppermute | solution.py:24
  168.2 65.1 %while.31 = (s32[]{:T(128)}, f32[3,416]{1,0:T(4,128)S(1)}, s32[32,128]{1,0:T(8,128)}, f32[3,416,128]{2,1,0:T(8,128)}, f32[3,416]{1,0:T(4,128)}, /*index=5*/f32[3...) while((s32[]{:T(128)}, f32[3,416]{1,0:T(4,128)S(1)}, ...), condition=%wide.region_18.19_spmd.clone, body=%wide.region_9.18_spmd.clone.sunk | while | flops 5704407040 | bytes 49676268 | solution.py:278
  176.6 2.8 %fusion.259 = (f32[2048,128]{1,0:T(8,128)S(1)}, f32[2048,128]{1,0:T(8,128)}, f32[2048,128]{1,0:T(8,128)}) fusion(f32[2048,256]{1,0:T(8,128)S(1)} %fusion.258, f32[2048]{0:T(1024)S(1)} %mul.917, f32[64,128]{1,0:T(8,128)S(1)} %dynamic-slice_convert_fusion.5, bf16[416,128]{1,0:T(8,128)(2,1)S(1)} %get-tuple-element.1076, s32[2048]{0:T(1024)S(1)} %eq.228), kind=kOutput, calls=%fused_computation.101.clone.1 | convolution fusion | flops 220266496 | bytes 4349952 | tf_op jit(solution)/shard_map/while/body/eval_jaxpr/dot_general | solution.py:165
  181.1 4.2 %fusion.261 = (f32[3,2048]{1,0:T(4,128)}, f32[2048,128]{0,1:T(8,128)}) fusion(f32[2048,128]{0,1:T(8,128)S(1)} %copy.98, f32[3,2048]{1,0:T(4,128)S(1)} %get-tuple-element.955, f32[3,416,128]{2,1,0:T(8,128)S(1)} %copy-done.22, s32[2048]{0:T(1024)S(1)} %eq.228), kind=kOutput, calls=%fused_computation.64.clone.1 | convolution fusion | flops 3929597952 | bytes 2793472 | tf_op jit(solution)/shard_map/while/body/eval_jaxpr/ne,kec->knc/dot_general | solution.py:271
  192.1 3.5 %fusion.263 = f32[2048,128]{1,0:T(8,128)S(1)} fusion(f32[2048,128]{1,0:T(8,128)S(1)} %get-tuple-element.961, f32[2048,128]{1,0:T(8,128)S(1)} %bitcast.242, f32[416,128]{1,0:T(8,128)S(1)} %copy-done.7, s32[2048]{0:T(1024)S(1)} %copy-done.15), kind=kOutput, calls=%fused_computation.69.clone.1 | convolution fusion | flops 1309999104 | bytes 3366912 | tf_op jit(solution)/shard_map/while/body/eval_jaxpr/ne,ec->nc/dot_general | solution.py:270
  209.0 2.8 %fusion.259 = (f32[2048,128]{1,0:T(8,128)S(1)}, f32[2048,128]{1,0:T(8,128)}, f32[2048,128]{1,0:T(8,128)}) fusion(f32[2048,256]{1,0:T(8,128)S(1)} %fusion.258, f32[2048]{0:T(1024)S(1)} %mul.917, f32[64,128]{1,0:T(8,128)S(1)} %dynamic-slice_convert_fusion.5, bf16[416,128]{1,0:T(8,128)(2,1)S(1)} %get-tuple-element.1076, s32[2048]{0:T(1024)S(1)} %eq.228), kind=kOutput, calls=%fused_computation.101.clone.1 | convolution fusion | flops 220266496 | bytes 4349952 | tf_op jit(solution)/shard_map/while/body/eval_jaxpr/dot_general | solution.py:165
  213.5 4.2 %fusion.261 = (f32[3,2048]{1,0:T(4,128)}, f32[2048,128]{0,1:T(8,128)}) fusion(f32[2048,128]{0,1:T(8,128)S(1)} %copy.98, f32[3,2048]{1,0:T(4,128)S(1)} %get-tuple-element.955, f32[3,416,128]{2,1,0:T(8,128)S(1)} %copy-done.22, s32[2048]{0:T(1024)S(1)} %eq.228), kind=kOutput, calls=%fused_computation.64.clone.1 | convolution fusion | flops 3929597952 | bytes 2793472 | tf_op jit(solution)/shard_map/while/body/eval_jaxpr/ne,kec->knc/dot_general | solution.py:271
  224.5 3.5 %fusion.263 = f32[2048,128]{1,0:T(8,128)S(1)} fusion(f32[2048,128]{1,0:T(8,128)S(1)} %get-tuple-element.961, f32[2048,128]{1,0:T(8,128)S(1)} %bitcast.242, f32[416,128]{1,0:T(8,128)S(1)} %copy-done.7, s32[2048]{0:T(1024)S(1)} %copy-done.15), kind=kOutput, calls=%fused_computation.69.clone.1 | convolution fusion | flops 1309999104 | bytes 3366912 | tf_op jit(solution)/shard_map/while/body/eval_jaxpr/ne,ec->nc/dot_general | solution.py:270
  239.1 5.6 %collective-permute-start.30 = (f32[3,32]{1,0:T(4,128)S(1)}, f32[3,32]{1,0:T(4,128)S(1)}, u32[]{:S(2)}, u32[]{:S(2)}) collective-permute-start(f32[3,32]{1,0:T(4,128)S(1)} %get-tuple-element.748), channel_id=1, source_target_pairs={{0,1},{1,2},{2,3},{3,0},{4,5},{5,6},{6,7},{7,4},{8,9},{9,10},{10,1... | collective-permute-start | bytes 1160 | tf_op jit(solution)/shard_map/ppermute | solution.py:14
  246.7 6.7 %collective-permute-start.27 = (f32[3,32]{1,0:T(4,128)S(1)}, f32[3,32]{1,0:T(4,128)S(1)}, u32[]{:S(2)}, u32[]{:S(2)}) collective-permute-start(f32[3,32]{1,0:T(4,128)S(1)} %get-tuple-element.750), channel_id=1, source_target_pairs={{0,508},{4,0},{8,4},{12,8},{16,12},{20,16},{24,20},{28,24},{32,28}... | collective-permute-start | bytes 1160 | tf_op jit(solution)/shard_map/ppermute | solution.py:14
  256.1 3.4 %collective-permute-start.26 = (f32[3,32]{1,0:T(4,128)S(1)}, f32[3,32]{1,0:T(4,128)S(1)}, u32[]{:S(2)}, u32[]{:S(2)}) collective-permute-start(f32[3,32]{1,0:T(4,128)S(1)} %get-tuple-element.751), channel_id=1, source_target_pairs={{0,508},{4,0},{8,4},{12,8},{16,12},{20,16},{24,20},{28,24},{32,28}... | collective-permute-start | bytes 1160 | tf_op jit(solution)/shard_map/ppermute | solution.py:14
  259.5 4.9 %collective-permute-start.35 = (f32[3,32]{1,0:T(4,128)S(1)}, f32[3,32]{1,0:T(4,128)S(1)}, u32[]{:S(2)}, u32[]{:S(2)}) collective-permute-start(f32[3,32]{1,0:T(4,128)S(1)} %collective-permute-done.34), channel_id=1, source_target_pairs={{0,1},{1,2},{2,3},{3,0},{4,5},{5,6},{6,7},{7,4},{8,9},{9,10},{10,1... | collective-permute-start | bytes 1160 | tf_op jit(solution)/shard_map/ppermute | solution.py:14
  266.3 5.1 %collective-permute-start.28 = (f32[3,32]{1,0:T(4,128)S(1)}, f32[3,32]{1,0:T(4,128)S(1)}, u32[]{:S(2)}, u32[]{:S(2)}) collective-permute-start(f32[3,32]{1,0:T(4,128)S(1)} %collective-permute-done.27), channel_id=1, source_target_pairs={{0,1},{1,2},{2,3},{3,0},{4,5},{5,6},{6,7},{7,4},{8,9},{9,10},{10,1... | collective-permute-start | bytes 1160 | tf_op jit(solution)/shard_map/ppermute | solution.py:14
  273.5 4.6 %collective-permute-done.25 = f32[3,32]{1,0:T(4,128)S(1)} collective-permute-done((f32[3,32]{1,0:T(4,128)S(1)}, f32[3,32]{1,0:T(4,128)S(1)}, u32[]{:S(2)}, u32[]{:S(2)}) %collective-permute-start.25) | collective-permute-done | bytes 416 | tf_op jit(solution)/shard_map/ppermute | solution.py:14
  (364 shorter events, 132.9 us)
Async XLA Ops:
  3.3 28.0 %collective-permute-start.1 = (f32[1,1,3,32]{3,2,1,0:T(4,128)S(1)}, f32[1,1,3,32]{3,2,1,0:T(4,128)S(1)}, u32[]{:S(2)}, u32[]{:S(2)}) collective-permute-start(f32[1,1,3,32]{3,2,1,0:T(4,128)S(1)} %bitcast.261), channel_id=1, source_target_pairs={{4,0},{8,4},{12,8},{16,12},{20,16},{24,20},{28,24},{32,28},{36,32}... | collective-permute-start | bytes 1160 | tf_op jit(solution)/shard_map/ppermute | solution.py:25
  16.6 14.7 %collective-permute-start = (f32[1,1,3,32]{3,2,1,0:T(4,128)S(1)}, f32[1,1,3,32]{3,2,1,0:T(4,128)S(1)}, u32[]{:S(2)}, u32[]{:S(2)}) collective-permute-start(f32[1,1,3,32]{3,2,1,0:T(4,128)S(1)} %bitcast.262), channel_id=1, source_target_pairs={{0,4},{4,8},{8,12},{12,16},{16,20},{20,24},{24,28},{28,32},{32,36}... | collective-permute-start | bytes 1160 | tf_op jit(solution)/shard_map/ppermute | solution.py:24
  21.3 18.5 %collective-permute-start.5 = (bf16[1,1,32,128]{3,2,1,0:T(8,128)(2,1)S(1)}, bf16[1,1,32,128]{3,2,1,0:T(8,128)(2,1)S(1)}, u32[]{:S(2)}, u32[]{:S(2)}) collective-permute-start(bf16[1,1,32,128]{3,2,1,0:T(8,128)(2,1)S(1)} %bitcast.253), channel_id=1, source_target_pairs={{4,0},{8,4},{12,8},{16,12},{20,16},{24,20},{28,24},{32,28},{36,32}... | collective-permute-start | bytes 24584 | tf_op jit(solution)/shard_map/ppermute | solution.py:25
  28.3 11.6 %collective-permute-start.4 = (bf16[1,1,32,128]{3,2,1,0:T(8,128)(2,1)S(1)}, bf16[1,1,32,128]{3,2,1,0:T(8,128)(2,1)S(1)}, u32[]{:S(2)}, u32[]{:S(2)}) collective-permute-start(bf16[1,1,32,128]{3,2,1,0:T(8,128)(2,1)S(1)} %bitcast.254), channel_id=1, source_target_pairs={{0,4},{4,8},{8,12},{12,16},{16,20},{20,24},{24,28},{28,32},{32,36}... | collective-permute-start | bytes 24584 | tf_op jit(solution)/shard_map/ppermute | solution.py:24
  31.3 8.3 %collective-permute-start.3 = (f32[3,1,3,32]{3,2,1,0:T(4,128)S(1)}, f32[3,1,3,32]{3,2,1,0:T(4,128)S(1)}, u32[]{:S(2)}, u32[]{:S(2)}) collective-permute-start(f32[3,1,3,32]{3,2,1,0:T(4,128)S(1)} %pad_maximum_fusion.9), channel_id=1, source_target_pairs={{1,0},{2,1},{3,2},{0,3},{5,4},{6,5},{7,6},{4,7},{9,8},{10,9},{11,1... | collective-permute-start | bytes 3464 | tf_op jit(solution)/shard_map/ppermute | solution.py:25
  39.9 7.9 %collective-permute-start.7 = (bf16[3,1,32,128]{3,2,1,0:T(8,128)(2,1)S(1)}, bf16[3,1,32,128]{3,2,1,0:T(8,128)(2,1)S(1)}, u32[]{:S(2)}, u32[]{:S(2)}) collective-permute-start(bf16[3,1,32,128]{3,2,1,0:T(8,128)(2,1)S(1)} %pad_maximum_fusion.8), channel_id=1, source_target_pairs={{1,0},{2,1},{3,2},{0,3},{5,4},{6,5},{7,6},{4,7},{9,8},{10,9},{11,1... | collective-permute-start | bytes 73736 | tf_op jit(solution)/shard_map/ppermute | solution.py:25
  91.5 13.1 %collective-permute-start.18 = (f32[4,32,128]{2,1,0:T(8,128)S(1)}, f32[4,32,128]{2,1,0:T(8,128)S(1)}, u32[]{:S(2)}, u32[]{:S(2)}) collective-permute-start(f32[4,32,128]{2,1,0:T(8,128)S(1)} %get-tuple-element.742), channel_id=1, source_target_pairs={{0,4},{4,8},{8,12},{12,16},{16,20},{20,24},{24,28},{28,32},{32,36}... | collective-permute-start | bytes 196616 | tf_op jit(solution)/shard_map/ppermute | solution.py:14
  93.4 17.9 %collective-permute-start.17 = (f32[4,32,128]{2,1,0:T(8,128)S(1)}, f32[4,32,128]{2,1,0:T(8,128)S(1)}, u32[]{:S(2)}, u32[]{:S(2)}) collective-permute-start(f32[4,32,128]{2,1,0:T(8,128)S(1)} %get-tuple-element.743), channel_id=1, source_target_pairs={{0,4},{4,8},{8,12},{12,16},{16,20},{20,24},{24,28},{28,32},{32,36}... | collective-permute-start | bytes 196616 | tf_op jit(solution)/shard_map/ppermute | solution.py:14
  95.3 18.7 %collective-permute-start.15 = (f32[4,32,128]{2,1,0:T(8,128)S(1)}, f32[4,32,128]{2,1,0:T(8,128)S(1)}, u32[]{:S(2)}, u32[]{:S(2)}) collective-permute-start(f32[4,32,128]{2,1,0:T(8,128)S(1)} %get-tuple-element.741), channel_id=1, source_target_pairs={{0,4},{4,8},{8,12},{12,16},{16,20},{20,24},{24,28},{28,32},{32,36}... | collective-permute-start | bytes 196616 | tf_op jit(solution)/shard_map/ppermute | solution.py:14
  97.2 20.1 %collective-permute-start.14 = (f32[4,32,128]{2,1,0:T(8,128)S(1)}, f32[4,32,128]{2,1,0:T(8,128)S(1)}, u32[]{:S(2)}, u32[]{:S(2)}) collective-permute-start(f32[4,32,128]{2,1,0:T(8,128)S(1)} %get-tuple-element.740), channel_id=1, source_target_pairs={{0,1},{1,2},{2,3},{3,0},{4,5},{5,6},{6,7},{7,4},{8,9},{9,10},{10,1... | collective-permute-start | bytes 196616 | tf_op jit(solution)/shard_map/ppermute | solution.py:14
  102.7 19.6 %collective-permute-start.13 = (f32[4,32,128]{2,1,0:T(8,128)S(1)}, f32[4,32,128]{2,1,0:T(8,128)S(1)}, u32[]{:S(2)}, u32[]{:S(2)}) collective-permute-start(f32[4,32,128]{2,1,0:T(8,128)S(1)} %get-tuple-element.739), channel_id=1, source_target_pairs={{0,3},{1,0},{2,1},{3,2},{4,7},{5,4},{6,5},{7,6},{8,11},{9,8},{10,9... | collective-permute-start | bytes 196616 | tf_op jit(solution)/shard_map/ppermute | solution.py:14
  104.6 19.6 %collective-permute-start.11 = (f32[4,32,128]{2,1,0:T(8,128)S(1)}, f32[4,32,128]{2,1,0:T(8,128)S(1)}, u32[]{:S(2)}, u32[]{:S(2)}) collective-permute-start(f32[4,32,128]{2,1,0:T(8,128)S(1)} %get-tuple-element.738), channel_id=1, source_target_pairs={{0,508},{4,0},{8,4},{12,8},{16,12},{20,16},{24,20},{28,24},{32,28}... | collective-permute-start | bytes 196616 | tf_op jit(solution)/shard_map/ppermute | solution.py:14
  111.3 18.0 %collective-permute-start.8 = (f32[4,32,128]{2,1,0:T(8,128)S(1)}, f32[4,32,128]{2,1,0:T(8,128)S(1)}, u32[]{:S(2)}, u32[]{:S(2)}) collective-permute-start(f32[4,32,128]{2,1,0:T(8,128)S(1)} %get-tuple-element.736), channel_id=1, source_target_pairs={{0,508},{4,0},{8,4},{12,8},{16,12},{20,16},{24,20},{28,24},{32,28}... | collective-permute-start | bytes 196616 | tf_op jit(solution)/shard_map/ppermute | solution.py:14
  114.0 17.8 %collective-permute-start.10 = (f32[4,32,128]{2,1,0:T(8,128)S(1)}, f32[4,32,128]{2,1,0:T(8,128)S(1)}, u32[]{:S(2)}, u32[]{:S(2)}) collective-permute-start(f32[4,32,128]{2,1,0:T(8,128)S(1)} %get-tuple-element.737), channel_id=1, source_target_pairs={{0,508},{4,0},{8,4},{12,8},{16,12},{20,16},{24,20},{28,24},{32,28}... | collective-permute-start | bytes 196616 | tf_op jit(solution)/shard_map/ppermute | solution.py:14
  117.4 14.5 %collective-permute-start.19 = (f32[4,32,128]{2,1,0:T(8,128)S(1)}, f32[4,32,128]{2,1,0:T(8,128)S(1)}, u32[]{:S(2)}, u32[]{:S(2)}) collective-permute-start(f32[4,32,128]{2,1,0:T(8,128)S(1)} %collective-permute-done.18), channel_id=1, source_target_pairs={{0,1},{1,2},{2,3},{3,0},{4,5},{5,6},{6,7},{7,4},{8,9},{9,10},{10,1... | collective-permute-start | bytes 196616 | tf_op jit(solution)/shard_map/ppermute | solution.py:14
  122.3 9.6 %collective-permute-start.16 = (f32[4,32,128]{2,1,0:T(8,128)S(1)}, f32[4,32,128]{2,1,0:T(8,128)S(1)}, u32[]{:S(2)}, u32[]{:S(2)}) collective-permute-start(f32[4,32,128]{2,1,0:T(8,128)S(1)} %collective-permute-done.15), channel_id=1, source_target_pairs={{0,3},{1,0},{2,1},{3,2},{4,7},{5,4},{6,5},{7,6},{8,11},{9,8},{10,9... | collective-permute-start | bytes 196616 | tf_op jit(solution)/shard_map/ppermute | solution.py:14
  124.2 7.7 %collective-permute-start.12 = (f32[4,32,128]{2,1,0:T(8,128)S(1)}, f32[4,32,128]{2,1,0:T(8,128)S(1)}, u32[]{:S(2)}, u32[]{:S(2)}) collective-permute-start(f32[4,32,128]{2,1,0:T(8,128)S(1)} %collective-permute-done.11), channel_id=1, source_target_pairs={{0,1},{1,2},{2,3},{3,0},{4,5},{5,6},{6,7},{7,4},{8,9},{9,10},{10,1... | collective-permute-start | bytes 196616 | tf_op jit(solution)/shard_map/ppermute | solution.py:14
  129.4 7.4 %collective-permute-start.9 = (f32[4,32,128]{2,1,0:T(8,128)S(1)}, f32[4,32,128]{2,1,0:T(8,128)S(1)}, u32[]{:S(2)}, u32[]{:S(2)}) collective-permute-start(f32[4,32,128]{2,1,0:T(8,128)S(1)} %collective-permute-done.8), channel_id=1, source_target_pairs={{0,3},{1,0},{2,1},{3,2},{4,7},{5,4},{6,5},{7,6},{8,11},{9,8},{10,9... | collective-permute-start | bytes 196616 | tf_op jit(solution)/shard_map/ppermute | solution.py:14
  146.0 8.9 %collective-permute-start.20 = (f32[1,1,4,32,128]{4,2,3,1,0:T(4,128)S(1)}, f32[1,1,4,32,128]{4,2,3,1,0:T(4,128)S(1)}, u32[]{:S(2)}, u32[]{:S(2)}) collective-permute-start(f32[1,1,4,32,128]{4,2,3,1,0:T(4,128)S(1)} %maximum_bitcast_fusion), channel_id=1, source_target_pairs={{0,4},{4,8},{8,12},{12,16},{16,20},{20,24},{24,28},{28,32},{32,36}... | collective-permute-start | bytes 196616 | tf_op jit(solution)/shard_map/ppermute | solution.py:24
  154.9 8.8 %collective-permute-start.23 = (f32[3,1,4,32,128]{4,2,3,1,0:T(4,128)S(1)}, f32[3,1,4,32,128]{4,2,3,1,0:T(4,128)S(1)}, u32[]{:S(2)}, u32[]{:S(2)}) collective-permute-start(f32[3,1,4,32,128]{4,2,3,1,0:T(4,128)S(1)} %pad_maximum_fusion.3), channel_id=1, source_target_pairs={{1,0},{2,1},{3,2},{0,3},{5,4},{6,5},{7,6},{4,7},{9,8},{10,9},{11,1... | collective-permute-start | bytes 589832 | tf_op jit(solution)/shard_map/ppermute | solution.py:25
  156.9 8.3 %collective-permute-start.22 = (f32[3,1,4,32,128]{4,2,3,1,0:T(4,128)S(1)}, f32[3,1,4,32,128]{4,2,3,1,0:T(4,128)S(1)}, u32[]{:S(2)}, u32[]{:S(2)}) collective-permute-start(f32[3,1,4,32,128]{4,2,3,1,0:T(4,128)S(1)} %pad_maximum_fusion.3), channel_id=1, source_target_pairs={{0,1},{1,2},{2,3},{3,0},{4,5},{5,6},{6,7},{7,4},{8,9},{9,10},{10,1... | collective-permute-start | bytes 589832 | tf_op jit(solution)/shard_map/ppermute | solution.py:24
  233.3 13.3 %collective-permute-start.34 = (f32[3,32]{1,0:T(4,128)S(1)}, f32[3,32]{1,0:T(4,128)S(1)}, u32[]{:S(2)}, u32[]{:S(2)}) collective-permute-start(f32[3,32]{1,0:T(4,128)S(1)} %get-tuple-element.745), channel_id=1, source_target_pairs={{0,4},{4,8},{8,12},{12,16},{16,20},{20,24},{24,28},{28,32},{32,36}... | collective-permute-start | bytes 1160 | tf_op jit(solution)/shard_map/ppermute | solution.py:14
  235.3 18.1 %collective-permute-start.33 = (f32[3,32]{1,0:T(4,128)S(1)}, f32[3,32]{1,0:T(4,128)S(1)}, u32[]{:S(2)}, u32[]{:S(2)}) collective-permute-start(f32[3,32]{1,0:T(4,128)S(1)} %get-tuple-element.746), channel_id=1, source_target_pairs={{0,4},{4,8},{8,12},{12,16},{16,20},{20,24},{24,28},{28,32},{32,36}... | collective-permute-start | bytes 1160 | tf_op jit(solution)/shard_map/ppermute | solution.py:14
  237.2 18.9 %collective-permute-start.31 = (f32[3,32]{1,0:T(4,128)S(1)}, f32[3,32]{1,0:T(4,128)S(1)}, u32[]{:S(2)}, u32[]{:S(2)}) collective-permute-start(f32[3,32]{1,0:T(4,128)S(1)} %get-tuple-element.747), channel_id=1, source_target_pairs={{0,4},{4,8},{8,12},{12,16},{16,20},{20,24},{24,28},{28,32},{32,36}... | collective-permute-start | bytes 1160 | tf_op jit(solution)/shard_map/ppermute | solution.py:14
  239.1 20.3 %collective-permute-start.30 = (f32[3,32]{1,0:T(4,128)S(1)}, f32[3,32]{1,0:T(4,128)S(1)}, u32[]{:S(2)}, u32[]{:S(2)}) collective-permute-start(f32[3,32]{1,0:T(4,128)S(1)} %get-tuple-element.748), channel_id=1, source_target_pairs={{0,1},{1,2},{2,3},{3,0},{4,5},{5,6},{6,7},{7,4},{8,9},{9,10},{10,1... | collective-permute-start | bytes 1160 | tf_op jit(solution)/shard_map/ppermute | solution.py:14
  244.7 19.6 %collective-permute-start.29 = (f32[3,32]{1,0:T(4,128)S(1)}, f32[3,32]{1,0:T(4,128)S(1)}, u32[]{:S(2)}, u32[]{:S(2)}) collective-permute-start(f32[3,32]{1,0:T(4,128)S(1)} %get-tuple-element.749), channel_id=1, source_target_pairs={{0,3},{1,0},{2,1},{3,2},{4,7},{5,4},{6,5},{7,6},{8,11},{9,8},{10,9... | collective-permute-start | bytes 1160 | tf_op jit(solution)/shard_map/ppermute | solution.py:14
  246.7 19.6 %collective-permute-start.27 = (f32[3,32]{1,0:T(4,128)S(1)}, f32[3,32]{1,0:T(4,128)S(1)}, u32[]{:S(2)}, u32[]{:S(2)}) collective-permute-start(f32[3,32]{1,0:T(4,128)S(1)} %get-tuple-element.750), channel_id=1, source_target_pairs={{0,508},{4,0},{8,4},{12,8},{16,12},{20,16},{24,20},{28,24},{32,28}... | collective-permute-start | bytes 1160 | tf_op jit(solution)/shard_map/ppermute | solution.py:14
  253.4 18.0 %collective-permute-start.24 = (f32[3,32]{1,0:T(4,128)S(1)}, f32[3,32]{1,0:T(4,128)S(1)}, u32[]{:S(2)}, u32[]{:S(2)}) collective-permute-start(f32[3,32]{1,0:T(4,128)S(1)} %get-tuple-element.744), channel_id=1, source_target_pairs={{0,508},{4,0},{8,4},{12,8},{16,12},{20,16},{24,20},{28,24},{32,28}... | collective-permute-start | bytes 1160 | tf_op jit(solution)/shard_map/ppermute | solution.py:14
  256.1 17.4 %collective-permute-start.26 = (f32[3,32]{1,0:T(4,128)S(1)}, f32[3,32]{1,0:T(4,128)S(1)}, u32[]{:S(2)}, u32[]{:S(2)}) collective-permute-start(f32[3,32]{1,0:T(4,128)S(1)} %get-tuple-element.751), channel_id=1, source_target_pairs={{0,508},{4,0},{8,4},{12,8},{16,12},{20,16},{24,20},{28,24},{32,28}... | collective-permute-start | bytes 1160 | tf_op jit(solution)/shard_map/ppermute | solution.py:14
  259.5 14.0 %collective-permute-start.35 = (f32[3,32]{1,0:T(4,128)S(1)}, f32[3,32]{1,0:T(4,128)S(1)}, u32[]{:S(2)}, u32[]{:S(2)}) collective-permute-start(f32[3,32]{1,0:T(4,128)S(1)} %collective-permute-done.34), channel_id=1, source_target_pairs={{0,1},{1,2},{2,3},{3,0},{4,5},{5,6},{6,7},{7,4},{8,9},{9,10},{10,1... | collective-permute-start | bytes 1160 | tf_op jit(solution)/shard_map/ppermute | solution.py:14
  264.3 9.2 %collective-permute-start.32 = (f32[3,32]{1,0:T(4,128)S(1)}, f32[3,32]{1,0:T(4,128)S(1)}, u32[]{:S(2)}, u32[]{:S(2)}) collective-permute-start(f32[3,32]{1,0:T(4,128)S(1)} %collective-permute-done.31), channel_id=1, source_target_pairs={{0,3},{1,0},{2,1},{3,2},{4,7},{5,4},{6,5},{7,6},{8,11},{9,8},{10,9... | collective-permute-start | bytes 1160 | tf_op jit(solution)/shard_map/ppermute | solution.py:14
  266.3 7.2 %collective-permute-start.28 = (f32[3,32]{1,0:T(4,128)S(1)}, f32[3,32]{1,0:T(4,128)S(1)}, u32[]{:S(2)}, u32[]{:S(2)}) collective-permute-start(f32[3,32]{1,0:T(4,128)S(1)} %collective-permute-done.27), channel_id=1, source_target_pairs={{0,1},{1,2},{2,3},{3,0},{4,5},{5,6},{6,7},{7,4},{8,9},{9,10},{10,1... | collective-permute-start | bytes 1160 | tf_op jit(solution)/shard_map/ppermute | solution.py:14
  (70 other events, 494.9 us)
where the time goes:
time: 283 us; the launch traced here: 280 us
  starting transfers between devices  129 us (46%)
  matrix products  71.7 us (25%)
  local copies, waits for them, and re-layouts  30.4 us (11%)
  other arithmetic  25.5 us (9%)
  waiting for transfers between devices  20.1 us (7%)
    ppermute x24, starting transfers between devices, from_behind(): return lax.ppermute(value, axis, pairs)  79.5 us
    ppermute x6, starting transfers between devices, extended(): after = lax.ppermute(first, axis, down)  29.1 us
    ppermute x6, starting transfers between devices, extended(): before = lax.ppermute(last, axis, up)  20.7 us
    dot_general x4, matrix products, edge_tile(): jnp.dot(selector.astype(jnp.bfloat16), extended_projection, preferred_ele...  10.7 us
    ppermute x24, waiting for transfers between devices, from_behind(): return lax.ppermute(value, axis, pairs)  9.5 us
    ppermute x6, waiting for transfers between devices, extended(): before = lax.ppermute(last, axis, up)  8.89 us
    dot_general x4, matrix products, edge_tile(): jnp.einsum('ce,ne->cn', extended_coords, selector_wide, precision=exact)  8.65 us
    dot_general x2, matrix products, backward_round(): jnp.einsum('ne,kec->knc', selector_wide, ext_cot_v, precision=exact)  8.33 us
  transfers between devices with their start and end apart: 36, of which 6 were waited for; matrix products, arithmetic and copies ran while one was open for 2% of the time, Pallas kernels for 0%

commit v1 on v0

v1 whole, which is shorter than its diff:
```python
import functools

import jax
import jax.numpy as jnp
from jax import lax
from jax.experimental import pallas as pl
from jax.experimental.pallas import tpu as pltpu
from jax.sharding import PartitionSpec as P

MESH = pl.DeviceIdType.MESH
F32 = jnp.float32
LOW = jnp.bfloat16
ATOMS = 128
CHAN = 128
LIST = 32
SLOTS = 32
HIDDEN = 64
GHOST = 8 * LIST
ROWS = ATOMS + GHOST
EDGES = SLOTS * ATOMS
PER = 4
CHUNK = PER * ATOMS
BANDS = 4
BAND = CHAN // BANDS
SIDES = [(a, b) for a in (-1, 0, 1) for b in (-1, 0, 1) if (a, b) != (0, 0)]
NN = (((1,), (0,)), ((), ()))
NT = (((1,), (1,)), ((), ()))


def dot(a, b, dims=NN):
    return lax.dot_general(a, b, dims, preferred_element_type=F32)


def sigmoid(x):
    return 0.5 * jnp.tanh(0.5 * x) + 0.5


def column(row, n):
    down = lax.broadcasted_iota(jnp.int32, (n, n), 0)
    across = lax.broadcasted_iota(jnp.int32, (n, n), 1)
    return jnp.sum(jnp.where(down == across, row, 0.0), axis=1, keepdims=True)


def split(x):
    high = x.astype(LOW)
    return high, (x - high.astype(F32)).astype(LOW)


def lanes_of(c):
    return pl.ds(pl.multiple_of(c * CHUNK, CHUNK), CHUNK)


def kernel(
    n_dom,
    n_slab,
    features_hbm,
    positions_hbm,
    neighbours_hbm,
    mask_hbm,
    list_hbm,
    w_up_hbm,
    w1_hbm,
    w2_hbm,
    w3_hbm,
    w_a_hbm,
    w_b_hbm,
    w_o1_hbm,
    w_o2_hbm,
    energies_ref,
    forces_ref,
    features,
    positions,
    neighbours,
    mask,
    ghost_list,
    w_up,
    w1,
    w2,
    w3,
    w_a,
    w_b,
    w_o1,
    w_o2,
    ext,
    ext_t,
    own_pos,
    pick,
    alive,
    hot,
    w1_t,
    w2_t,
    w3_t,
    w_a_t,
    w_b_t,
    w_o1_t,
    features_t,
    proj_t,
    partner,
    unit,
    inverse,
    slope,
    gate1,
    gate2,
    radial,
    messages,
    agg,
    cot,
    cot_ext,
    partner_cot,
    d_radial,
    d_unit,
    d_rel,
    send1,
    send2,
    recv2,
    send3,
    recv3,
    send4,
    recv4,
    load_sem,
    out_sem,
    in_sem,
):
    dom = lax.axis_index("dom")
    slab = lax.axis_index("slab")
    peers = [
        (lax.rem(dom + a + n_dom, n_dom), lax.rem(slab + b + n_slab, n_slab)) for a, b in SIDES
    ]
    barrier = pltpu.get_barrier_semaphore()
    for peer in peers:
        pl.semaphore_signal(barrier, inc=1, device_id=peer, device_id_type=MESH)

    def push(phase, j, src, dst):
        return pltpu.make_async_remote_copy(
            src_ref=src,
            dst_ref=dst,
            send_sem=out_sem.at[phase, j],
            recv_sem=in_sem.at[phase, 7 - j],
            device_id=peers[j],
            device_id_type=MESH,
        )

    pairs = [
        (features_hbm, features),
        (w_up_hbm, w_up),
        (positions_hbm, positions),
        (list_hbm, ghost_list),
        (neighbours_hbm, neighbours),
        (mask_hbm, mask),
        (w1_hbm, w1),
        (w2_hbm, w2),
        (w3_hbm, w3),
        (w_a_hbm, w_a),
        (w_b_hbm, w_b),
        (w_o1_hbm, w_o1),
        (w_o2_hbm, w_o2),
    ]
    loads = [pltpu.make_async_copy(a, b, load_sem.at[i]) for i, (a, b) in enumerate(pairs)]
    for load in loads:
        load.start()
    for load in loads[:4]:
        load.wait()

    proj = dot(features[...], w_up[...]).astype(LOW)
    own_pos[...] = jnp.zeros_like(own_pos)
    own_pos[0:3, :] = positions[...]
    coords = own_pos[...]
    high = coords.astype(LOW).astype(F32)
    rest = coords - high
    middle = rest.astype(LOW).astype(F32)
    pieces = jnp.concatenate(
        [high, middle, rest - middle, jnp.zeros((CHAN - 24, ATOMS), F32)], axis=0
    )
    ext[0:ATOMS, 0:CHAN] = proj
    ext[0:ATOMS, CHAN : 2 * CHAN] = pieces.T.astype(LOW)
    list_column = column(ghost_list[...].astype(F32), LIST)
    atom_lane = lax.broadcasted_iota(jnp.int32, (LIST, ATOMS), 1).astype(F32)
    pick[...] = jnp.where(atom_lane == list_column, 1.0, 0.0).astype(LOW)
    send1[...] = dot(pick[...], ext[0:ATOMS, :]).astype(LOW)

    pl.semaphore_wait(barrier, 8)
    copies1 = [
        push(0, j, send1, ext.at[pl.ds(ATOMS + LIST * (7 - j), LIST), :]) for j in range(8)
    ]
    for copy in copies1:
        copy.start()

    for load in loads[4:]:
        load.wait()
    alive[...] = jnp.where(mask[...] != 0, 1.0 / 16.0, 0.0)
    row_number = lax.broadcasted_iota(jnp.int32, (ROWS, ATOMS), 0)

    def select(c, carry):
        for i in range(PER):
            entry = neighbours[pl.ds(c * PER + i, 1), :]
            entry = jnp.where(entry >= ATOMS + 5 * LIST, entry - LIST, entry)
            here = pl.ds(pl.multiple_of(c * CHUNK + i * ATOMS, ATOMS), ATOMS)
            hot[:, here] = jnp.where(row_number == entry, 1.0, 0.0).astype(LOW)
        return carry

    lax.fori_loop(0, SLOTS // PER, select, 0)
    w1_t[...] = jnp.concatenate(
        [w1[...].astype(F32), jnp.zeros((8, HIDDEN), F32)], axis=0
    ).T.astype(LOW)
    w2_t[...] = w2[...].astype(F32).T.astype(LOW)
    w3_t[...] = w3[...].astype(F32).T.astype(LOW)
    w_a_t[...] = w_a[...].astype(F32).T.astype(LOW)
    w_b_t[...] = w_b[...].astype(F32).T.astype(LOW)
    w_o1_t[...] = w_o1[...].astype(F32).T.astype(LOW)
    features_t[...] = features[...].astype(F32).T
    proj_t[...] = ext[0:ATOMS, 0:CHAN].astype(F32).T
    entry = lax.broadcasted_iota(jnp.int32, (8, ROWS), 1) - ATOMS
    axis = lax.broadcasted_iota(jnp.int32, (8, ROWS), 0)
    block = lax.div(entry + ATOMS, LIST) - ATOMS // LIST
    first = jnp.where(block < 3, -4.0, jnp.where(block > 4, 4.0, 0.0))
    left = (block == 0) | (block == 3) | (block == 5)
    right = (block == 2) | (block == 4) | (block == 7)
    second = jnp.where(left, -4.0, jnp.where(right, 4.0, 0.0))
    offset = jnp.where(axis == 0, first, jnp.where(axis == 1, second, 0.0))
    offset = jnp.where(entry < 0, 0.0, offset)

    for copy in copies1:
        copy.wait_recv()
    ext_t[0:CHAN, :] = ext[:, 0:CHAN].astype(F32).T.astype(LOW)
    pieces_t = ext[:, CHAN : 2 * CHAN].astype(F32).T
    ext_t[CHAN : CHAN + 32, :] = jnp.concatenate([pieces_t[0:24], offset], axis=0).astype(LOW)

    centre = 1.0 + 0.75 * lax.broadcasted_iota(jnp.int32, (8, CHUNK), 0).astype(F32)

    def forward(c, carry):
        here = lanes_of(c)
        found = dot(ext_t[...], hot[:, here])
        partner[:, here] = found[0:CHAN]
        place = found[CHAN : CHAN + 8] + found[CHAN + 8 : CHAN + 16] + found[CHAN + 16 : CHAN + 24]
        place = place + found[CHAN + 24 : CHAN + 32]
        rel = place - jnp.concatenate([own_pos[...]] * PER, axis=1)
        spread = jnp.sqrt(jnp.sum(rel * rel, axis=0, keepdims=True) + 1.0)
        inv = 1.0 / spread
        direction = rel * inv
        unit[:, here] = direction
        inverse[:, here] = jnp.broadcast_to(inv, (8, CHUNK))
        away = spread - centre
        basis = jnp.exp(-(away * away))
        slope[:, here] = -2.0 * away * basis
        wide = jnp.concatenate([basis, jnp.zeros((8, CHUNK), F32)], axis=0).astype(LOW)
        flags = jnp.concatenate([alive[pl.ds(c * PER + i, 1), :] for i in range(PER)], axis=1)
        pre1 = dot(w1_t[...], wide)
        open1 = sigmoid(pre1)
        gate1[:, here] = open1 * (1.0 + pre1 * (1.0 - open1))
        pre2 = dot(w2_t[...], (pre1 * open1).astype(LOW))
        open2 = sigmoid(pre2)
        gate2[:, here] = open2 * (1.0 + pre2 * (1.0 - open2)) * flags
        hid2 = ((pre2 * open2).astype(LOW).astype(F32) * flags).astype(LOW)
        radial[:, here] = dot(w3_t[...], hid2)
        for i in range(PER):
            tile = pl.ds(pl.multiple_of(c * CHUNK + i * ATOMS, ATOMS), ATOMS)
            toward = [-unit[k : k + 1, tile] for k in range(3)]
            for b in range(BANDS):
                rows = pl.ds(b * BAND, BAND)
                own = proj_t[rows, :]
                messages[rows, tile] = (radial[rows, tile] * own).astype(LOW)
                vector = radial[pl.ds(CHAN + b * BAND, BAND), tile] * own
                for k in range(3):
                    messages[pl.ds((k + 1) * CHAN + b * BAND, BAND), tile] = (
                        vector * toward[k]
                    ).astype(LOW)
        return carry

    lax.fori_loop(0, SLOTS // PER, forward, 0)

    send2[...] = dot(hot[ATOMS:ROWS, :], messages[...], NT).astype(LOW)
    copies2 = [
        push(1, j, send2.at[pl.ds(LIST * j, LIST), :], recv2.at[7 - j]) for j in range(8)
    ]
    for copy in copies2:
        copy.start()

    agg[...] = dot(messages[...], hot[0:ATOMS, :], NT)

    def gather_own(c, carry):
        for b in range(BANDS):
            rows = pl.ds(b * BAND, BAND)
            total = [agg[pl.ds(k * CHAN + b * BAND, BAND), :] for k in range(4)]
            for i in range(PER):
                tile = pl.ds(pl.multiple_of(c * CHUNK + i * ATOMS, ATOMS), ATOMS)
                other = partner[rows, tile]
                total[0] = total[0] + radial[rows, tile] * other
                vector = radial[pl.ds(CHAN + b * BAND, BAND), tile] * other
                for k in range(3):
                    total[k + 1] = total[k + 1] + vector * unit[k : k + 1, tile]
            for k in range(4):
                agg[pl.ds(k * CHAN + b * BAND, BAND), :] = total[k]
        return carry

    lax.fori_loop(0, SLOTS // PER, gather_own, 0)

    for copy in copies2:
        copy.wait_recv()
    back = recv2[0].astype(F32)
    for j in range(1, 8):
        back = back + recv2[j].astype(F32)
    twice = jnp.concatenate([pick[...], pick[...]], axis=0)
    agg[...] += dot(jnp.concatenate(split(back.T), axis=1), twice)

    along = [agg[(k + 1) * CHAN : (k + 2) * CHAN, :] for k in range(3)]
    norms = along[0] * along[0] + along[1] * along[1] + along[2] * along[2]
    mixed = features_t[...] + dot(w_a_t[...], agg[0:CHAN, :].astype(LOW))
    mixed = mixed + dot(w_b_t[...], norms.astype(LOW))
    pre = dot(w_o1_t[...], mixed.astype(LOW))
    opened = sigmoid(pre)
    out_weight = column(w_o2[...], 16)
    energies_ref[...] = jnp.sum(pre * opened * out_weight, axis=0, keepdims=True)
    d_pre = out_weight * opened * (1.0 + pre * (1.0 - opened))
    d_mixed = dot(w_o1[...], d_pre.astype(LOW)).astype(LOW)
    cot[0:CHAN, :] = dot(w_a[...], d_mixed).astype(LOW)
    d_norms = 2.0 * dot(w_b[...], d_mixed).astype(LOW).astype(F32)
    for k in range(3):
        cot[(k + 1) * CHAN : (k + 2) * CHAN, :] = (along[k] * d_norms).astype(LOW)
    send3[...] = dot(pick[...], cot[...], NT).astype(LOW)
    copies3 = [push(2, j, send3, recv3.at[pl.ds(LIST * (7 - j), LIST), :]) for j in range(8)]
    for copy in copies3:
        copy.start()
    cot_ext[:, 0:ATOMS] = cot[...]
    for copy in copies3:
        copy.wait_recv()
    cot_ext[:, ATOMS:ROWS] = recv3[...].astype(F32).T.astype(LOW)

    def backward(c, carry):
        here = lanes_of(c)
        partner_cot[...] = dot(cot_ext[...], hot[:, here])
        for i in range(PER):
            tile = pl.ds(pl.multiple_of(c * CHUNK + i * ATOMS, ATOMS), ATOMS)
            inner = pl.ds(i * ATOMS, ATOMS)
            toward = [unit[k : k + 1, tile] for k in range(3)]
            sums = [jnp.zeros((8, ATOMS), F32) for k in range(3)]
            for b in range(BANDS):
                rows = pl.ds(b * BAND, BAND)
                own = proj_t[rows, :]
                other = partner[rows, tile]
                weight = radial[pl.ds(CHAN + b * BAND, BAND), tile]
                d_radial[rows, inner] = (
                    other * cot[rows, :].astype(F32) + own * partner_cot[rows, inner]
                ).astype(LOW)
                flow = jnp.zeros((BAND, ATOMS), F32)
                for k in range(3):
                    part = pl.ds((k + 1) * CHAN + b * BAND, BAND)
                    term = other * cot[part, :].astype(F32) - own * partner_cot[part, inner]
                    flow = flow + toward[k] * term
                    pull = weight * term
                    for r in range(BAND // 8):
                        sums[k] = sums[k] + pull[8 * r : 8 * r + 8]
                d_radial[pl.ds(CHAN + b * BAND, BAND), inner] = flow.astype(LOW)
            for k in range(3):
                d_unit[k : k + 1, inner] = jnp.sum(sums[k], axis=0, keepdims=True)
        d_hid2 = dot(w3[...], d_radial[...])
        d_hid1 = dot(w2[...], (d_hid2 * gate2[:, here]).astype(LOW))
        d_basis = dot(w1[...], (d_hid1 * gate1[:, here]).astype(LOW))
        d_spread = jnp.sum(d_basis * slope[:, here], axis=0, keepdims=True)
        direction = unit[:, here]
        pull = d_unit[...]
        inv = inverse[:, here]
        radial_part = jnp.sum(pull * direction, axis=0, keepdims=True)
        change = (pull - direction * radial_part) * inv + direction * d_spread
        total = carry
        for i in range(PER):
            total = total + change[:, i * ATOMS : (i + 1) * ATOMS]
        d_rel[:, here] = jnp.concatenate(
            [change, change - change.astype(LOW).astype(F32)], axis=0
        ).astype(LOW)
        return total

    d_unit[...] = jnp.zeros_like(d_unit)
    force = lax.fori_loop(0, SLOTS // PER, backward, jnp.zeros((8, ATOMS), F32))

    away = dot(d_rel[...], hot[ATOMS:ROWS, :], NT)
    send4[...] = away[0:8] + away[8:16]
    copies4 = [push(3, j, send4, recv4.at[7 - j]) for j in range(8)]
    for copy in copies4:
        copy.start()
    near = dot(d_rel[...], hot[0:ATOMS, :], NT)
    force = force - (near[0:8] + near[8:16])
    for copy in copies4:
        copy.wait_recv()
    back = recv4[0][:, 7 * LIST : 8 * LIST]
    for j in range(1, 8):
        back = back + recv4[j][:, (7 - j) * LIST : (8 - j) * LIST]
    force = force - dot(jnp.concatenate(split(back), axis=1), twice)
    forces_ref[...] = force[0:3]
    for copy in copies1 + copies2 + copies3 + copies4:
        copy.wait_send()


def body(
    n_dom,
    n_slab,
    features,
    positions,
    neighbours,
    neighbour_mask,
    ghost_list,
    w_up,
    radial_weight_1,
    radial_weight_2,
    radial_weight_3,
    w_a,
    w_b,
    w_o1,
    w_o2,
):
    operands = (
        features,
        positions,
        neighbours,
        neighbour_mask,
        ghost_list.reshape(1, LIST),
        w_up,
        radial_weight_1,
        radial_weight_2,
        radial_weight_3,
        w_a,
        w_b,
        w_o1,
        w_o2.reshape(1, 16),
    )
    held = [pltpu.VMEM(x.shape, x.dtype) for x in operands]
    energies, forces = pl.pallas_call(
        functools.partial(kernel, n_dom, n_slab),
        out_shape=(
            jax.ShapeDtypeStruct((1, ATOMS), F32),
            jax.ShapeDtypeStruct((3, ATOMS), F32),
        ),
        in_specs=[pl.BlockSpec(memory_space=pl.ANY)] * len(operands),
        out_specs=(
            pl.BlockSpec(memory_space=pltpu.VMEM),
            pl.BlockSpec(memory_space=pltpu.VMEM),
        ),
        scratch_shapes=held
        + [
            pltpu.VMEM((ROWS, 2 * CHAN), LOW),
            pltpu.VMEM((CHAN + 32, ROWS), LOW),
            pltpu.VMEM((8, ATOMS), F32),
            pltpu.VMEM((LIST, ATOMS), LOW),
            pltpu.VMEM((SLOTS, ATOMS), F32),
            pltpu.VMEM((ROWS, EDGES), LOW),
            pltpu.VMEM((HIDDEN, 16), LOW),
            pltpu.VMEM((HIDDEN, HIDDEN), LOW),
            pltpu.VMEM((2 * CHAN, HIDDEN), LOW),
            pltpu.VMEM((CHAN, CHAN), LOW),
            pltpu.VMEM((CHAN, CHAN), LOW),
            pltpu.VMEM((16, CHAN), LOW),
            pltpu.VMEM((CHAN, ATOMS), F32),
            pltpu.VMEM((CHAN, ATOMS), F32),
            pltpu.VMEM((CHAN, EDGES), F32),
            pltpu.VMEM((8, EDGES), F32),
            pltpu.VMEM((8, EDGES), F32),
            pltpu.VMEM((8, EDGES), F32),
            pltpu.VMEM((HIDDEN, EDGES), F32),
            pltpu.VMEM((HIDDEN, EDGES), F32),
            pltpu.VMEM((2 * CHAN, EDGES), F32),
            pltpu.VMEM((4 * CHAN, EDGES), LOW),
            pltpu.VMEM((4 * CHAN, ATOMS), F32),
            pltpu.VMEM((4 * CHAN, ATOMS), LOW),
            pltpu.VMEM((4 * CHAN, ROWS), LOW),
            pltpu.VMEM((4 * CHAN, CHUNK), F32),
            pltpu.VMEM((2 * CHAN, CHUNK), LOW),
            pltpu.VMEM((8, CHUNK), F32),
            pltpu.VMEM((16, EDGES), LOW),
            pltpu.VMEM((LIST, 2 * CHAN), LOW),
            pltpu.VMEM((GHOST, 4 * CHAN), LOW),
            pltpu.VMEM((8, LIST, 4 * CHAN), LOW),
            pltpu.VMEM((LIST, 4 * CHAN), LOW),
            pltpu.VMEM((GHOST, 4 * CHAN), LOW),
            pltpu.VMEM((8, GHOST), F32),
            pltpu.VMEM((8, 8, GHOST), F32),
            pltpu.SemaphoreType.DMA((13,)),
            pltpu.SemaphoreType.DMA((4, 8)),
            pltpu.SemaphoreType.DMA((4, 8)),
        ],
        compiler_params=pltpu.CompilerParams(
            collective_id=0, has_side_effects=True, vmem_limit_bytes=48 * 1024 * 1024
        ),
    )(*operands)
    return energies.reshape(ATOMS), forces


def solution(mesh):
    split_rows = P(("dom", "slab"), None)
    split_lanes = P(None, ("dom", "slab"))
    split_flat = P(("dom", "slab"))
    in_specs = (split_rows, split_lanes, split_lanes, split_lanes, split_flat) + (P(),) * 8
    return jax.shard_map(
        functools.partial(body, mesh.shape["dom"], mesh.shape["slab"]),
        mesh=mesh,
        in_specs=in_specs,
        out_specs=(split_flat, split_lanes),
        check_vma=False,
    )
```

time: 283 us -> 63.4 us (0.22)
  starting transfers between devices: 129 us -> 0 us
  matrix products: 71.7 us -> 0 us
  Pallas kernels: 0 us -> 54.7 us
  other arithmetic: 25.5 us -> 0 us
  local copies, waits for them, and re-layouts: 30.4 us -> 7.12 us
  waiting for transfers between devices: 20.1 us -> 0 us
    ppermute x36 -> x0, starting transfers between devices: 129 us -> none  [the longest x24 79.5 us: from_behind(): return lax.ppermute(value, axis, pairs)]
    dot_general x38 -> x0, matrix products: 71.7 us -> none  [the longest x4 10.7 us: edge_tile(): jnp.dot(selector.astype(jnp.bfloat16), extended_projection, preferred_ele...]
    pallas_call x0 -> x1, Pallas kernels: none -> 54.7 us  [body(): pl.pallas_call(functools.partial(kernel, n_dom, n_slab), out_shape=(jax.S...]
    ppermute x36 -> x0, waiting for transfers between devices: 20.1 us -> none  [the longest x24 9.5 us: from_behind(): return lax.ppermute(value, axis, pairs)]
    dynamic_slice x12 -> x0, local copies, waits for them, and re-layouts: 8.18 us -> none  [the longest x4 3.18 us: edge_tile(): lax.dynamic_slice_in_dim(neighbours, start_offset, rows_of_width, 1)]
    reduce_sum x11 -> x0, other arithmetic: 7.38 us -> none  [the longest x2 5 us: pair_messages(): direction[:, :, None] * (vector_weight * partner_wide)[None]]
    while x109 -> x0, local copies, waits for them, and re-layouts: 4.35 us -> none
    gather x5 -> x0, local copies, waits for them, and re-layouts: 4.25 us -> none  [the longest x1 1.53 us: body(): cot_s[ghost_list][None]]
  transfers between devices with their start and end apart: 36 -> 0, of which waited for: 6 -> 0; matrix products, arithmetic and copies ran while one was open for 2% -> 0% of each run, Pallas kernels for 0% -> 0%
where the time goes in v1:
time: 63.4 us; the launch traced here: 62.5 us
  Pallas kernels  54.7 us (86%)
  local copies, waits for them, and re-layouts  7.12 us (11%)
  between operations  0.73 us (1%)
    pallas_call x1, Pallas kernels, body(): pl.pallas_call(functools.partial(kernel, n_dom, n_slab), out_shape=(jax.S...  54.7 us
    unnamed x27, local copies, waits for them, and re-layouts  7.12 us

profile of v1, /device:TPU:6, one launch (start us, length us, event | category | flops | bytes accessed | tf_op | source)
XLA Modules:
  0.0 62.5 jit_solution(832432716199700463)
XLA Ops:
  0.6 0.0 copy-start
  0.6 0.0 copy-start.8
  0.7 0.0 copy-start.9
  0.7 0.0 copy-start.10
  0.7 0.0 copy-start.11
  0.7 0.8 %copy.15.w_o1_hbm = bf16[128,16]{1,0:T(8,128)(2,1)S(1)} copy(bf16[128,16]{0,1:T(8,128)(2,1)} %param.24) | data formatting | bytes 8192 | tf_op args[11]
  1.5 0.0 copy-done
  1.5 0.0 copy-done.8
  1.5 0.0 copy-done.9
  1.5 0.0 copy-done.10
  1.5 0.0 copy-done.11
  1.6 0.0 copy-start.1
  1.6 0.7 %copy-done.1 = bf16[128,128]{1,0:T(8,128)(2,1)S(1)} copy-done((bf16[128,128]{1,0:T(8,128)(2,1)S(1)}, bf16[128,128]{1,0:T(8,128)(2,1)}, u32[]{:S(2)}) %copy-start.1) | copy-done | bytes 32792
  2.3 0.0 copy-start.2
  2.3 0.8 %copy-done.2 = bf16[64,256]{1,0:T(8,128)(2,1)S(1)} copy-done((bf16[64,256]{1,0:T(8,128)(2,1)S(1)}, bf16[64,256]{1,0:T(8,128)(2,1)}, u32[]{:S(2)}) %copy-start.2) | copy-done | bytes 32792
  3.1 0.0 copy-start.3
  3.1 0.8 %copy-done.3 = bf16[128,128]{1,0:T(8,128)(2,1)S(1)} copy-done((bf16[128,128]{1,0:T(8,128)(2,1)S(1)}, bf16[128,128]{1,0:T(8,128)(2,1)}, u32[]{:S(2)}) %copy-start.3) | copy-done | bytes 32792
  3.8 0.0 copy-start.4
  3.8 0.8 %copy-done.4 = bf16[128,128]{1,0:T(8,128)(2,1)S(1)} copy-done((bf16[128,128]{1,0:T(8,128)(2,1)S(1)}, bf16[128,128]{1,0:T(8,128)(2,1)}, u32[]{:S(2)}) %copy-start.4) | copy-done | bytes 32792
  4.6 0.0 copy-start.5
  4.6 0.7 %copy-done.5 = s32[32,128]{1,0:T(8,128)S(1)} copy-done((s32[32,128]{1,0:T(8,128)S(1)}, s32[32,128]{1,0:T(8,128)}, u32[]{:S(2)}) %copy-start.5) | copy-done | bytes 16408
  5.3 0.0 copy-start.6
  5.3 0.7 %copy-done.6 = s32[32,128]{1,0:T(8,128)S(1)} copy-done((s32[32,128]{1,0:T(8,128)S(1)}, s32[32,128]{1,0:T(8,128)}, u32[]{:S(2)}) %copy-start.6) | copy-done | bytes 16408
  6.0 0.0 copy-start.7
  6.0 0.7 %copy-done.7 = bf16[64,64]{1,0:T(8,128)(2,1)S(1)} copy-done((bf16[64,64]{1,0:T(8,128)(2,1)S(1)}, bf16[64,64]{1,0:T(8,128)(2,1)}, u32[]{:S(2)}) %copy-start.7) | copy-done | bytes 8216
  6.7 54.7 %shard_map.140 = (f32[1,128]{1,0:T(1,128)S(1)}, f32[3,128]{1,0:T(4,128)S(1)}) custom-call(bf16[128,128]{1,0:T(8,128)(2,1)S(1)} %copy-done, f32[3,128]{1,0:T(4,128)S(1)} %copy-done.8, s32[32,128]{1,0:T(8,128)S(1)} %copy-done.5, s32[32,128]{1,0:T(8,128)S(1)} %copy-done.6, s32[1,32]{1,0:T(1,128)S(1)} %bitcast.3, bf16[128,128]{1,0:T(8,128)(2,1)S(1)} %copy-done.1, ...), custom_call_target="tpu_custom_call" | custom-call | tf_op jit(solution)/shard_map/pallas_call | solution.py:426
  61.4 0.5 copy.18
  62.0 0.6 copy.19
Async XLA Ops:
  0.6 0.9 %copy-start = (bf16[128,128]{1,0:T(8,128)(2,1)S(1)}, bf16[128,128]{1,0:T(8,128)(2,1)}, u32[]{:S(2)}) copy-start(bf16[128,128]{1,0:T(8,128)(2,1)} %features_hbm.1) | copy-start | bytes 98308
  0.6 0.9 %copy-start.8 = (f32[3,128]{1,0:T(4,128)S(1)}, f32[3,128]{1,0:T(4,128)}, u32[]{:S(2)}) copy-start(f32[3,128]{1,0:T(4,128)} %positions_hbm.1) | copy-start | bytes 4612
  0.7 0.9 %copy-start.9 = (bf16[8,64]{1,0:T(8,128)(2,1)S(1)}, bf16[8,64]{1,0:T(8,128)(2,1)}, u32[]{:S(2)}) copy-start(bf16[8,64]{1,0:T(8,128)(2,1)} %w1_hbm.1) | copy-start | bytes 3076
  0.7 0.9 %copy-start.10 = (s32[32]{0:T(128)S(1)}, s32[32]{0:T(128)}, u32[]{:S(2)}) copy-start(s32[32]{0:T(128)} %param.17) | copy-start | bytes 388
  0.7 0.9 %copy-start.11 = (f32[16]{0:T(128)S(1)}, f32[16]{0:T(128)}, u32[]{:S(2)}) copy-start(f32[16]{0:T(128)} %param.25) | copy-start | bytes 196
  1.6 0.8 %copy-start.1 = (bf16[128,128]{1,0:T(8,128)(2,1)S(1)}, bf16[128,128]{1,0:T(8,128)(2,1)}, u32[]{:S(2)}) copy-start(bf16[128,128]{1,0:T(8,128)(2,1)} %w_up_hbm.1) | copy-start | bytes 98308
  2.3 0.8 %copy-start.2 = (bf16[64,256]{1,0:T(8,128)(2,1)S(1)}, bf16[64,256]{1,0:T(8,128)(2,1)}, u32[]{:S(2)}) copy-start(bf16[64,256]{1,0:T(8,128)(2,1)} %w3_hbm.1) | copy-start | bytes 98308
  3.1 0.8 %copy-start.3 = (bf16[128,128]{1,0:T(8,128)(2,1)S(1)}, bf16[128,128]{1,0:T(8,128)(2,1)}, u32[]{:S(2)}) copy-start(bf16[128,128]{1,0:T(8,128)(2,1)} %w_a_hbm.1) | copy-start | bytes 98308
  3.8 0.8 %copy-start.4 = (bf16[128,128]{1,0:T(8,128)(2,1)S(1)}, bf16[128,128]{1,0:T(8,128)(2,1)}, u32[]{:S(2)}) copy-start(bf16[128,128]{1,0:T(8,128)(2,1)} %w_b_hbm.1) | copy-start | bytes 98308
  4.6 0.7 %copy-start.5 = (s32[32,128]{1,0:T(8,128)S(1)}, s32[32,128]{1,0:T(8,128)}, u32[]{:S(2)}) copy-start(s32[32,128]{1,0:T(8,128)} %neighbours_hbm.1) | copy-start | bytes 49156
  5.3 0.7 %copy-start.6 = (s32[32,128]{1,0:T(8,128)S(1)}, s32[32,128]{1,0:T(8,128)}, u32[]{:S(2)}) copy-start(s32[32,128]{1,0:T(8,128)} %mask_hbm.1) | copy-start | bytes 49156
  6.0 0.7 %copy-start.7 = (bf16[64,64]{1,0:T(8,128)(2,1)S(1)}, bf16[64,64]{1,0:T(8,128)(2,1)}, u32[]{:S(2)}) copy-start(bf16[64,64]{1,0:T(8,128)(2,1)} %w2_hbm.1) | copy-start | bytes 24580

commit v2 on v1

v2 whole, which is shorter than its diff:
```python
import functools

import jax
import jax.numpy as jnp
from jax import lax
from jax.experimental import pallas as pl
from jax.experimental.pallas import tpu as pltpu
from jax.sharding import PartitionSpec as P

MESH = pl.DeviceIdType.MESH
F32 = jnp.float32
LOW = jnp.bfloat16
ATOMS = 128
CHAN = 128
LIST = 32
SLOTS = 32
HIDDEN = 64
GHOST = 8 * LIST
ROWS = ATOMS + GHOST
EDGES = SLOTS * ATOMS
BANDS = 4
BAND = CHAN // BANDS
SIDES = [(a, b) for a in (-1, 0, 1) for b in (-1, 0, 1) if (a, b) != (0, 0)]
ORDER = (0, 2, 5, 7, 1, 6, 3, 4)
NN = (((1,), (0,)), ((), ()))
NT = (((1,), (1,)), ((), ()))


def dot(a, b, dims=NN):
    return lax.dot_general(a, b, dims, preferred_element_type=F32)


def sigmoid(x):
    return 0.5 * jnp.tanh(0.5 * x) + 0.5


def column(row, n):
    down = lax.broadcasted_iota(jnp.int32, (n, n), 0)
    across = lax.broadcasted_iota(jnp.int32, (n, n), 1)
    return jnp.sum(jnp.where(down == across, row, 0.0), axis=1, keepdims=True)


def split(x):
    high = x.astype(LOW)
    return high, (x - high.astype(F32)).astype(LOW)


def tile_of(i):
    return pl.ds(i * ATOMS, ATOMS)


def band(part, b):
    return pl.ds(part * CHAN + b * BAND, BAND)


def fold(x):
    total = x[0:8]
    for r in range(1, x.shape[0] // 8):
        total = total + x[8 * r : 8 * r + 8]
    return total


def kernel(
    n_dom,
    n_slab,
    features_hbm,
    positions_hbm,
    neighbours_hbm,
    mask_hbm,
    list_hbm,
    w_up_hbm,
    w1_hbm,
    w2_hbm,
    w3_hbm,
    w_a_hbm,
    w_b_hbm,
    w_o1_hbm,
    w_o2_hbm,
    energies_ref,
    forces_ref,
    features,
    positions,
    neighbours,
    mask,
    ghost_list,
    w_up,
    w1,
    w2,
    w3,
    w_a,
    w_b,
    w_o1,
    w_o2,
    ext,
    ext_t,
    own_pos,
    pick,
    pick8,
    alive,
    hot,
    w1_t,
    w2_t,
    w3_t,
    w_a_t,
    w_b_t,
    w_o1_t,
    features_t,
    proj_t,
    near_found,
    partner,
    unit,
    inverse,
    slope,
    gate1,
    gate2,
    radial,
    d_radial,
    messages,
    agg,
    cot,
    own_cot,
    partner_cot,
    factors,
    partial,
    send1,
    send2,
    recv2,
    send3,
    recv3,
    send4,
    recv4,
    load_sem,
    out_sem,
    in_sem,
):
    dom = lax.axis_index("dom")
    slab = lax.axis_index("slab")
    peers = [
        (lax.rem(dom + a + n_dom, n_dom), lax.rem(slab + b + n_slab, n_slab)) for a, b in SIDES
    ]
    barrier = pltpu.get_barrier_semaphore()
    for peer in peers:
        pl.semaphore_signal(barrier, inc=1, device_id=peer, device_id_type=MESH)

    def push(phase, j, src, dst):
        return pltpu.make_async_remote_copy(
            src_ref=src,
            dst_ref=dst,
            send_sem=out_sem.at[phase, j],
            recv_sem=in_sem.at[phase, 7 - j],
            device_id=peers[j],
            device_id_type=MESH,
        )

    pairs = [
        (features_hbm, features),
        (w_up_hbm, w_up),
        (positions_hbm, positions),
        (list_hbm, ghost_list),
        (neighbours_hbm, neighbours),
        (mask_hbm, mask),
        (w1_hbm, w1),
        (w2_hbm, w2),
        (w3_hbm, w3),
        (w_a_hbm, w_a),
        (w_b_hbm, w_b),
        (w_o1_hbm, w_o1),
        (w_o2_hbm, w_o2),
    ]
    loads = [pltpu.make_async_copy(a, b, load_sem.at[i]) for i, (a, b) in enumerate(pairs)]
    for load in loads:
        load.start()
    for load in loads[:4]:
        load.wait()

    proj = dot(features[...], w_up[...]).astype(LOW)
    own_pos[...] = jnp.zeros_like(own_pos)
    own_pos[0:3, :] = positions[...]
    coords = own_pos[...]
    high = coords.astype(LOW).astype(F32)
    rest = coords - high
    middle = rest.astype(LOW).astype(F32)
    pieces = jnp.concatenate(
        [high, middle, rest - middle, jnp.zeros((CHAN - 24, ATOMS), F32)], axis=0
    )
    ext[0:ATOMS, 0:CHAN] = proj
    ext[0:ATOMS, CHAN : 2 * CHAN] = pieces.T.astype(LOW)
    list_column = column(ghost_list[...].astype(F32), LIST)
    atom_lane = lax.broadcasted_iota(jnp.int32, (LIST, ATOMS), 1).astype(F32)
    pick[...] = jnp.where(atom_lane == list_column, 1.0, 0.0).astype(LOW)
    send1[...] = dot(pick[...], ext[0:ATOMS, :]).astype(LOW)

    for load in loads[4:]:
        load.wait()
    alive[...] = jnp.where(mask[...] != 0, 1.0 / 16.0, 0.0)
    row_number = lax.broadcasted_iota(jnp.int32, (ROWS, ATOMS), 0)
    for i in range(SLOTS):
        entry = neighbours[i : i + 1, :]
        entry = jnp.where(entry >= ATOMS + 5 * LIST, entry - LIST, entry)
        hot[:, tile_of(i)] = jnp.where(row_number == entry, 1.0, 0.0).astype(LOW)
    w1_t[...] = jnp.concatenate(
        [w1[...].astype(F32), jnp.zeros((8, HIDDEN), F32)], axis=0
    ).T.astype(LOW)
    w2_t[...] = w2[...].astype(F32).T.astype(LOW)
    w3_t[...] = w3[...].astype(F32).T.astype(LOW)
    w_a_t[...] = w_a[...].astype(F32).T.astype(LOW)
    w_b_t[...] = w_b[...].astype(F32).T.astype(LOW)
    w_o1_t[...] = w_o1[...].astype(F32).T.astype(LOW)
    features_t[...] = features[...].astype(F32).T
    own_t = ext[0:ATOMS, :].astype(F32).T
    proj_t[...] = own_t[0:CHAN]
    ext_t[:, 0:ATOMS] = own_t[0 : CHAN + 32].astype(LOW)

    pl.semaphore_wait(barrier, 8)
    copies1 = [
        push(0, j, send1, ext.at[pl.ds(ATOMS + LIST * (7 - j), LIST), :]) for j in range(8)
    ]
    for j in ORDER:
        copies1[j].start()

    near_found[...] = dot(ext_t[:, 0:ATOMS], hot[0:ATOMS, :])
    entry = lax.broadcasted_iota(jnp.int32, (8, GHOST), 1)
    axis = lax.broadcasted_iota(jnp.int32, (8, GHOST), 0)
    block = lax.div(entry, LIST)
    first = jnp.where(block < 3, -4.0, jnp.where(block > 4, 4.0, 0.0))
    left = (block == 0) | (block == 3) | (block == 5)
    right = (block == 2) | (block == 4) | (block == 7)
    second = jnp.where(left, -4.0, jnp.where(right, 4.0, 0.0))
    offset = jnp.where(axis == 0, first, jnp.where(axis == 1, second, 0.0))
    flags = jnp.concatenate([alive[i : i + 1, :] for i in range(SLOTS)], axis=1)
    centre = 1.0 + 0.75 * lax.broadcasted_iota(jnp.int32, (8, EDGES), 0).astype(F32)
    pick8[...] = jnp.concatenate([pick[...]] * 8, axis=0)

    for copy in copies1:
        copy.wait_recv()
    ghost_t = ext[ATOMS:ROWS, :].astype(F32).T
    ext_t[:, ATOMS:ROWS] = jnp.concatenate([ghost_t[0 : CHAN + 24], offset], axis=0).astype(LOW)

    found = near_found[...] + dot(ext_t[:, ATOMS:ROWS], hot[ATOMS:ROWS, :])
    partner[...] = found[0:CHAN]
    place = found[CHAN : CHAN + 8] + found[CHAN + 8 : CHAN + 16] + found[CHAN + 16 : CHAN + 24]
    place = place + found[CHAN + 24 : CHAN + 32]
    rel = place - jnp.concatenate([own_pos[...]] * SLOTS, axis=1)
    spread = jnp.sqrt(jnp.sum(rel * rel, axis=0, keepdims=True) + 1.0)
    inv = 1.0 / spread
    unit[...] = rel * inv
    inverse[...] = jnp.broadcast_to(inv, (8, EDGES))
    away = spread - centre
    basis = jnp.exp(-(away * away))
    slope[...] = -2.0 * away * basis
    blank = jnp.zeros((8, EDGES), F32)
    pre1 = dot(w1_t[...], jnp.concatenate([basis, blank], axis=0).astype(LOW))
    open1 = sigmoid(pre1)
    gate1[...] = open1 * (1.0 + pre1 * (1.0 - open1))
    pre2 = dot(w2_t[...], (pre1 * open1).astype(LOW))
    open2 = sigmoid(pre2)
    gate2[...] = open2 * (1.0 + pre2 * (1.0 - open2)) * flags
    hid2 = ((pre2 * open2).astype(LOW).astype(F32) * flags).astype(LOW)
    radial[...] = dot(w3_t[...], hid2)
    for i in range(SLOTS):
        tile = tile_of(i)
        toward = [-unit[k : k + 1, tile] for k in range(3)]
        for b in range(BANDS):
            own = proj_t[band(0, b), :]
            messages[band(0, b), tile] = (radial[band(0, b), tile] * own).astype(LOW)
            vector = radial[band(1, b), tile] * own
            for k in range(3):
                messages[band(k + 1, b), tile] = (vector * toward[k]).astype(LOW)

    send2[...] = dot(hot[ATOMS:ROWS, :], messages[...], NT).astype(LOW)
    copies2 = [
        push(1, j, send2.at[pl.ds(LIST * j, LIST), :], recv2.at[pl.ds(LIST * (7 - j), LIST), :])
        for j in range(8)
    ]
    for j in ORDER:
        copies2[j].start()

    agg[...] = dot(messages[...], hot[0:ATOMS, :], NT)
    for b in range(BANDS):
        total = [agg[band(k, b), :] for k in range(4)]
        for i in range(SLOTS):
            tile = tile_of(i)
            other = partner[band(0, b), tile]
            total[0] = total[0] + radial[band(0, b), tile] * other
            vector = radial[band(1, b), tile] * other
            for k in range(3):
                total[k + 1] = total[k + 1] + vector * unit[k : k + 1, tile]
        for k in range(4):
            agg[band(k, b), :] = total[k]
    rate = dot(w1_t[...], jnp.concatenate([slope[...], blank], axis=0).astype(LOW))
    rate = dot(w2_t[...], (rate * gate1[...]).astype(LOW))
    d_radial[...] = dot(w3_t[...], (rate * gate2[...]).astype(LOW))

    for copy in copies2:
        copy.wait_recv()
    back = recv2[0:LIST, :].astype(F32)
    for j in range(1, 8):
        back = back + recv2[LIST * j : LIST * (j + 1), :].astype(F32)
    agg[...] += dot(jnp.concatenate(split(back.T), axis=1), pick8[0 : 2 * LIST, :])

    along = [agg[(k + 1) * CHAN : (k + 2) * CHAN, :] for k in range(3)]
    norms = along[0] * along[0] + along[1] * along[1] + along[2] * along[2]
    mixed = features_t[...] + dot(w_a_t[...], agg[0:CHAN, :].astype(LOW))
    mixed = mixed + dot(w_b_t[...], norms.astype(LOW))
    pre = dot(w_o1[...], mixed.astype(LOW))
    opened = sigmoid(pre)
    out_weight = column(w_o2[...], 16)
    energies_ref[...] = jnp.sum(pre * opened * out_weight, axis=0, keepdims=True)
    d_pre = out_weight * opened * (1.0 + pre * (1.0 - opened))
    d_mixed = dot(w_o1_t[...], d_pre.astype(LOW)).astype(LOW)
    cot[0:CHAN, :] = dot(w_a[...], d_mixed).astype(LOW)
    d_norms = 2.0 * dot(w_b[...], d_mixed).astype(LOW).astype(F32)
    for k in range(3):
        cot[(k + 1) * CHAN : (k + 2) * CHAN, :] = (along[k] * d_norms).astype(LOW)
    send3[...] = dot(pick[...], cot[...], NT).astype(LOW)
    copies3 = [push(2, j, send3, recv3.at[pl.ds(LIST * (7 - j), LIST), :]) for j in range(8)]
    for j in ORDER:
        copies3[j].start()

    partner_cot[...] = dot(cot[...], hot[0:ATOMS, :])
    own_cot[...] = cot[...].astype(F32)
    for i in range(SLOTS):
        tile = tile_of(i)
        toward = [unit[k : k + 1, tile] for k in range(3)]
        sums = [jnp.zeros((8, ATOMS), F32) for k in range(4)]
        for b in range(BANDS):
            own = proj_t[band(0, b), :]
            other = partner[band(0, b), tile]
            weight = radial[band(1, b), tile]
            rate_s = d_radial[band(0, b), tile]
            rate_v = d_radial[band(1, b), tile]
            term = other * own_cot[band(0, b), :] + own * partner_cot[band(0, b), tile]
            spread_part = rate_s * term
            flow = jnp.zeros((BAND, ATOMS), F32)
            for k in range(3):
                term = other * own_cot[band(k + 1, b), :] - own * partner_cot[band(k + 1, b), tile]
                flow = flow + toward[k] * term
                sums[k + 1] = sums[k + 1] + fold(weight * term)
            sums[0] = sums[0] + fold(spread_part + rate_v * flow)
            factors[band(0, b), tile] = rate_s * own
            factors[band(1, b), tile] = rate_v * own
            factors[band(2, b), tile] = weight * own
        for k in range(4):
            partial[8 * k : 8 * k + 8, tile] = sums[k]

    for copy in copies3:
        copy.wait_recv()
    ghost_cot = recv3[...].astype(F32).T.astype(LOW)
    partner_cot[...] = dot(ghost_cot, hot[ATOMS:ROWS, :])
    for i in range(SLOTS):
        tile = tile_of(i)
        toward = [unit[k : k + 1, tile] for k in range(3)]
        sums = [partial[8 * k : 8 * k + 8, tile] for k in range(4)]
        for b in range(BANDS):
            weight = factors[band(2, b), tile]
            flow = jnp.zeros((BAND, ATOMS), F32)
            for k in range(3):
                far = partner_cot[band(k + 1, b), tile]
                flow = flow + toward[k] * far
                sums[k + 1] = sums[k + 1] - fold(weight * far)
            spread_part = factors[band(0, b), tile] * partner_cot[band(0, b), tile]
            sums[0] = sums[0] + fold(spread_part - factors[band(1, b), tile] * flow)
        for k in range(4):
            partial[8 * k : 8 * k + 8, tile] = sums[k]
    whole = [jnp.sum(partial[8 * k : 8 * k + 8, :], axis=0, keepdims=True) for k in range(4)]
    direction = unit[...]
    place_row = lax.broadcasted_iota(jnp.int32, (8, EDGES), 0)
    pull = jnp.where(
        place_row == 0,
        whole[1],
        jnp.where(place_row == 1, whole[2], jnp.where(place_row == 2, whole[3], 0.0)),
    )
    lengthwise = jnp.sum(pull * direction, axis=0, keepdims=True)
    change = (pull - direction * lengthwise) * inverse[...] + direction * whole[0]
    high, low = split(change)
    d_rel = jnp.concatenate([high.astype(F32), low.astype(F32)], axis=0).astype(LOW)

    parted = dot(d_rel, hot[ATOMS:ROWS, :], NT)
    send4[...] = parted[0:8] + parted[8:16]
    copies4 = [push(3, j, send4, recv4.at[7 - j]) for j in range(8)]
    for j in ORDER:
        copies4[j].start()
    near = dot(d_rel, hot[0:ATOMS, :], NT)
    force = -(near[0:8] + near[8:16])
    for i in range(SLOTS):
        force = force + change[:, i * ATOMS : (i + 1) * ATOMS]
    for copy in copies4:
        copy.wait_recv()
    lane_block = lax.div(lax.broadcasted_iota(jnp.int32, (8, GHOST), 1), LIST)
    back = recv4[0]
    for j in range(1, 8):
        back = jnp.where(lane_block == 7 - j, recv4[j], back)
    high, low = split(back)
    given = jnp.concatenate([high.astype(F32), low.astype(F32)], axis=0).astype(LOW)
    given = dot(given, pick8[...])
    force = force - (given[0:8] + given[8:16])
    forces_ref[...] = force[0:3]
    for copy in copies1 + copies2 + copies3 + copies4:
        copy.wait_send()


def body(
    n_dom,
    n_slab,
    features,
    positions,
    neighbours,
    neighbour_mask,
    ghost_list,
    w_up,
    radial_weight_1,
    radial_weight_2,
    radial_weight_3,
    w_a,
    w_b,
    w_o1,
    w_o2,
):
    operands = (
        features,
        positions,
        neighbours,
        neighbour_mask,
        ghost_list.reshape(1, LIST),
        w_up,
        radial_weight_1,
        radial_weight_2,
        radial_weight_3,
        w_a,
        w_b,
        w_o1.T,
        w_o2.reshape(1, 16),
    )
    held = [pltpu.VMEM(x.shape, x.dtype) for x in operands]
    energies, forces = pl.pallas_call(
        functools.partial(kernel, n_dom, n_slab),
        out_shape=(
            jax.ShapeDtypeStruct((1, ATOMS), F32),
            jax.ShapeDtypeStruct((3, ATOMS), F32),
        ),
        in_specs=[pl.BlockSpec(memory_space=pltpu.HBM)] * len(operands),
        out_specs=(
            pl.BlockSpec(memory_space=pltpu.VMEM),
            pl.BlockSpec(memory_space=pltpu.VMEM),
        ),
        scratch_shapes=held
        + [
            pltpu.VMEM((ROWS, 2 * CHAN), LOW),
            pltpu.VMEM((CHAN + 32, ROWS), LOW),
            pltpu.VMEM((8, ATOMS), F32),
            pltpu.VMEM((LIST, ATOMS), LOW),
            pltpu.VMEM((GHOST, ATOMS), LOW),
            pltpu.VMEM((SLOTS, ATOMS), F32),
            pltpu.VMEM((ROWS, EDGES), LOW),
            pltpu.VMEM((HIDDEN, 16), LOW),
            pltpu.VMEM((HIDDEN, HIDDEN), LOW),
            pltpu.VMEM((2 * CHAN, HIDDEN), LOW),
            pltpu.VMEM((CHAN, CHAN), LOW),
            pltpu.VMEM((CHAN, CHAN), LOW),
            pltpu.VMEM((CHAN, 16), LOW),
            pltpu.VMEM((CHAN, ATOMS), F32),
            pltpu.VMEM((CHAN, ATOMS), F32),
            pltpu.VMEM((CHAN + 32, EDGES), F32),
            pltpu.VMEM((CHAN, EDGES), F32),
            pltpu.VMEM((8, EDGES), F32),
            pltpu.VMEM((8, EDGES), F32),
            pltpu.VMEM((8, EDGES), F32),
            pltpu.VMEM((HIDDEN, EDGES), F32),
            pltpu.VMEM((HIDDEN, EDGES), F32),
            pltpu.VMEM((2 * CHAN, EDGES), F32),
            pltpu.VMEM((2 * CHAN, EDGES), F32),
            pltpu.VMEM((4 * CHAN, EDGES), LOW),
            pltpu.VMEM((4 * CHAN, ATOMS), F32),
            pltpu.VMEM((4 * CHAN, ATOMS), LOW),
            pltpu.VMEM((4 * CHAN, ATOMS), F32),
            pltpu.VMEM((4 * CHAN, EDGES), F32),
            pltpu.VMEM((3 * CHAN, EDGES), F32),
            pltpu.VMEM((32, EDGES), F32),
            pltpu.VMEM((LIST, 2 * CHAN), LOW),
            pltpu.VMEM((GHOST, 4 * CHAN), LOW),
            pltpu.VMEM((GHOST, 4 * CHAN), LOW),
            pltpu.VMEM((LIST, 4 * CHAN), LOW),
            pltpu.VMEM((GHOST, 4 * CHAN), LOW),
            pltpu.VMEM((8, GHOST), F32),
            pltpu.VMEM((8, 8, GHOST), F32),
            pltpu.SemaphoreType.DMA((13,)),
            pltpu.SemaphoreType.DMA((4, 8)),
            pltpu.SemaphoreType.DMA((4, 8)),
        ],
        compiler_params=pltpu.CompilerParams(
            collective_id=0, has_side_effects=True, vmem_limit_bytes=64 * 1024 * 1024
        ),
    )(*operands)
    return energies.reshape(ATOMS), forces


def solution(mesh):
    split_rows = P(("dom", "slab"), None)
    split_lanes = P(None, ("dom", "slab"))
    split_flat = P(("dom", "slab"))
    in_specs = (split_rows, split_lanes, split_lanes, split_lanes, split_flat) + (P(),) * 8
    return jax.shard_map(
        functools.partial(body, mesh.shape["dom"], mesh.shape["slab"]),
        mesh=mesh,
        in_specs=in_specs,
        out_specs=(split_flat, split_lanes),
        check_vma=False,
    )
```

time: 63.4 us -> 45.6 us (0.72)
  Pallas kernels: 54.7 us -> 42.9 us
  local copies, waits for them, and re-layouts: 7.12 us -> 1.71 us
    pallas_call x1, Pallas kernels: 54.7 us -> 42.9 us  [body(): pl.pallas_call(functools.partial(kernel, n_dom, n_slab), out_shape=(jax.S...]
    unnamed x27 -> x6, local copies, waits for them, and re-layouts: 7.12 us -> 1.71 us
where the time goes in v2:
time: 45.6 us; the launch traced here: 45.3 us
  Pallas kernels  42.9 us (94%)
  local copies, waits for them, and re-layouts  1.71 us (4%)
  between operations  0.66 us (1%)
    pallas_call x1, Pallas kernels, body(): pl.pallas_call(functools.partial(kernel, n_dom, n_slab), out_shape=(jax.S...  42.9 us
    unnamed x6, local copies, waits for them, and re-layouts  1.71 us

profile of v2, /device:TPU:6, one launch (start us, length us, event | category | flops | bytes accessed | tf_op | source)
XLA Modules:
  0.0 45.3 jit_solution(2865597434565785635)
XLA Ops:
  0.6 42.9 %shard_map.140 = (f32[1,128]{1,0:T(1,128)}, f32[3,128]{1,0:T(4,128)}) custom-call(bf16[128,128]{1,0:T(8,128)(2,1)} %features_hbm.1, f32[3,128]{1,0:T(4,128)} %positions_hbm.1, s32[32,128]{1,0:T(8,128)} %neighbours_hbm.1, s32[32,128]{1,0:T(8,128)} %mask_hbm.1, s32[1,32]{1,0:T(1,128)} %bitcast.5, bf16[128,128]{1,0:T(8,128)(2,1)} %w_up_hbm.1, ...), custom_call_target="tpu_custom_call" | custom-call | tf_op jit(solution)/shard_map/pallas_call | solution.py:435
  43.5 0.0 copy-start.1
  43.5 0.0 copy-start
  43.5 0.6 %copy-done.1 = f32[1,128]{1,0:T(1,128)S(1)} copy-done((f32[1,128]{1,0:T(1,128)S(1)}, f32[1,128]{1,0:T(1,128)}, u32[]{:S(2)}) %copy-start.1) | copy-done | bytes 536
  44.2 0.5 %copy.17 = f32[128]{0:T(128)} copy(f32[128]{0:T(128)S(1)} %bitcast.7) | data formatting | bytes 1024
  44.7 0.0 copy-done
  44.7 0.6 %copy.18 = f32[3,128]{1,0:T(4,128)} copy(f32[3,128]{1,0:T(4,128)S(1)} %copy-done) | data formatting | bytes 3072
Async XLA Ops:
  43.5 0.6 %copy-start.1 = (f32[1,128]{1,0:T(1,128)S(1)}, f32[1,128]{1,0:T(1,128)}, u32[]{:S(2)}) copy-start(f32[1,128]{1,0:T(1,128)} %get-tuple-element.4) | copy-start | bytes 1540
  43.5 1.1 %copy-start = (f32[3,128]{1,0:T(4,128)S(1)}, f32[3,128]{1,0:T(4,128)}, u32[]{:S(2)}) copy-start(f32[3,128]{1,0:T(4,128)} %get-tuple-element.9) | copy-start | bytes 4612

commit v3 on v2

--- a/solution.py
+++ b/solution.py
@@ -32,6 +32,11 @@
 
 def sigmoid(x):
     return 0.5 * jnp.tanh(0.5 * x) + 0.5
+
+
+def slope_of(x):
+    opened = sigmoid(x)
+    return opened * (1.0 + x * (1.0 - opened))
 
 
 def column(row, n):
@@ -101,10 +106,10 @@
     w1_t,
     w2_t,
     w3_t,
-    w_a_t,
-    w_b_t,
-    w_o1_t,
-    features_t,
+    fold_rows,
+    fold_columns,
+    own_pre,
+    out_weight,
     proj_t,
     near_found,
     partner,
@@ -203,10 +208,6 @@
     ).T.astype(LOW)
     w2_t[...] = w2[...].astype(F32).T.astype(LOW)
     w3_t[...] = w3[...].astype(F32).T.astype(LOW)
-    w_a_t[...] = w_a[...].astype(F32).T.astype(LOW)
-    w_b_t[...] = w_b[...].astype(F32).T.astype(LOW)
-    w_o1_t[...] = w_o1[...].astype(F32).T.astype(LOW)
-    features_t[...] = features[...].astype(F32).T
     own_t = ext[0:ATOMS, :].astype(F32).T
     proj_t[...] = own_t[0:CHAN]
     ext_t[:, 0:ATOMS] = own_t[0 : CHAN + 32].astype(LOW)
@@ -218,7 +219,14 @@
     for j in ORDER:
         copies1[j].start()
 
-    near_found[...] = dot(ext_t[:, 0:ATOMS], hot[0:ATOMS, :])
+    folded = jnp.concatenate([dot(w_o1[...], w_a[...], NT), dot(w_o1[...], w_b[...], NT)], axis=1)
+    high, low = split(folded)
+    folded = jnp.concatenate([high.astype(F32), low.astype(F32)], axis=0)
+    fold_rows[...] = folded.astype(LOW)
+    fold_columns[...] = folded.T.astype(LOW)
+    own_pre[...] = dot(w_o1[...], features[...], NT)
+    out_weight[...] = column(w_o2[...], 16)
+    near_found[...] = dot(ext_t[CHAN : CHAN + 32, 0:ATOMS], hot[0:ATOMS, :])
     entry = lax.broadcasted_iota(jnp.int32, (8, GHOST), 1)
     axis = lax.broadcasted_iota(jnp.int32, (8, GHOST), 0)
     block = lax.div(entry, LIST)
@@ -236,25 +244,23 @@
     ghost_t = ext[ATOMS:ROWS, :].astype(F32).T
     ext_t[:, ATOMS:ROWS] = jnp.concatenate([ghost_t[0 : CHAN + 24], offset], axis=0).astype(LOW)
 
-    found = near_found[...] + dot(ext_t[:, ATOMS:ROWS], hot[ATOMS:ROWS, :])
-    partner[...] = found[0:CHAN]
-    place = found[CHAN : CHAN + 8] + found[CHAN + 8 : CHAN + 16] + found[CHAN + 16 : CHAN + 24]
-    place = place + found[CHAN + 24 : CHAN + 32]
-    rel = place - jnp.concatenate([own_pos[...]] * SLOTS, axis=1)
-    spread = jnp.sqrt(jnp.sum(rel * rel, axis=0, keepdims=True) + 1.0)
-    inv = 1.0 / spread
-    unit[...] = rel * inv
-    inverse[...] = jnp.broadcast_to(inv, (8, EDGES))
+    found = near_found[...] + dot(ext_t[CHAN : CHAN + 32, ATOMS:ROWS], hot[ATOMS:ROWS, :])
+    place = found[0:8] + found[8:16] + found[16:24] + found[24:32]
+    unit[...] = place - jnp.concatenate([own_pos[...]] * SLOTS, axis=1)
+    rel = [jnp.broadcast_to(unit[k : k + 1, :], (8, EDGES)) for k in range(3)]
+    spread = jnp.sqrt(rel[0] * rel[0] + rel[1] * rel[1] + rel[2] * rel[2] + 1.0)
+    inverse[...] = 1.0 / spread
+    unit[...] = unit[...] * inverse[...]
     away = spread - centre
     basis = jnp.exp(-(away * away))
     slope[...] = -2.0 * away * basis
     blank = jnp.zeros((8, EDGES), F32)
     pre1 = dot(w1_t[...], jnp.concatenate([basis, blank], axis=0).astype(LOW))
     open1 = sigmoid(pre1)
-    gate1[...] = open1 * (1.0 + pre1 * (1.0 - open1))
+    gate1[...] = pre1
     pre2 = dot(w2_t[...], (pre1 * open1).astype(LOW))
     open2 = sigmoid(pre2)
-    gate2[...] = open2 * (1.0 + pre2 * (1.0 - open2)) * flags
+    gate2[...] = pre2
     hid2 = ((pre2 * open2).astype(LOW).astype(F32) * flags).astype(LOW)
     radial[...] = dot(w3_t[...], hid2)
     for i in range(SLOTS):
@@ -275,6 +281,7 @@
     for j in ORDER:
         copies2[j].start()
 
+    partner[...] = dot(ext_t[0:CHAN, :], hot[...])
     agg[...] = dot(messages[...], hot[0:ATOMS, :], NT)
     for b in range(BANDS):
         total = [agg[band(k, b), :] for k in range(4)]
@@ -288,8 +295,9 @@
         for k in range(4):
             agg[band(k, b), :] = total[k]
     rate = dot(w1_t[...], jnp.concatenate([slope[...], blank], axis=0).astype(LOW))
-    rate = dot(w2_t[...], (rate * gate1[...]).astype(LOW))
-    d_radial[...] = dot(w3_t[...], (rate * gate2[...]).astype(LOW))
+    rate = dot(w2_t[...], (rate * slope_of(gate1[...])).astype(LOW))
+    rate = rate * slope_of(gate2[...]) * flags
+    d_radial[...] = dot(w3_t[...], rate.astype(LOW))
 
     for copy in copies2:
         copy.wait_recv()
@@ -300,16 +308,16 @@
 
     along = [agg[(k + 1) * CHAN : (k + 2) * CHAN, :] for k in range(3)]
     norms = along[0] * along[0] + along[1] * along[1] + along[2] * along[2]
-    mixed = features_t[...] + dot(w_a_t[...], agg[0:CHAN, :].astype(LOW))
-    mixed = mixed + dot(w_b_t[...], norms.astype(LOW))
-    pre = dot(w_o1[...], mixed.astype(LOW))
+    lowered = jnp.concatenate([agg[0:CHAN, :].astype(LOW), norms.astype(LOW)], axis=0)
+    pre = dot(fold_rows[...], lowered)
+    pre = pre[0:16] + pre[16:32] + own_pre[...]
     opened = sigmoid(pre)
-    out_weight = column(w_o2[...], 16)
-    energies_ref[...] = jnp.sum(pre * opened * out_weight, axis=0, keepdims=True)
-    d_pre = out_weight * opened * (1.0 + pre * (1.0 - opened))
-    d_mixed = dot(w_o1_t[...], d_pre.astype(LOW)).astype(LOW)
-    cot[0:CHAN, :] = dot(w_a[...], d_mixed).astype(LOW)
-    d_norms = 2.0 * dot(w_b[...], d_mixed).astype(LOW).astype(F32)
+    energies_ref[...] = jnp.sum(pre * opened * out_weight[...], axis=0, keepdims=True)
+    d_pre = out_weight[...] * opened * (1.0 + pre * (1.0 - opened))
+    d_pre = d_pre.astype(LOW)
+    back = dot(fold_columns[...], jnp.concatenate([d_pre, d_pre], axis=0))
+    cot[0:CHAN, :] = back[0:CHAN].astype(LOW)
+    d_norms = 2.0 * back[CHAN : 2 * CHAN]
     for k in range(3):
         cot[(k + 1) * CHAN : (k + 2) * CHAN, :] = (along[k] * d_norms).astype(LOW)
     send3[...] = dot(pick[...], cot[...], NT).astype(LOW)
@@ -362,16 +370,19 @@
             sums[0] = sums[0] + fold(spread_part - factors[band(1, b), tile] * flow)
         for k in range(4):
             partial[8 * k : 8 * k + 8, tile] = sums[k]
-    whole = [jnp.sum(partial[8 * k : 8 * k + 8, :], axis=0, keepdims=True) for k in range(4)]
-    direction = unit[...]
+    high, low = split(partial[...])
+    halves = jnp.concatenate([high, low], axis=0)
+    row = lax.broadcasted_iota(jnp.int32, (32, 64), 0)
+    across = lax.broadcasted_iota(jnp.int32, (32, 64), 1)
+    same = lax.div(row, 8) == lax.rem(lax.div(across, 8), 4)
+    whole = dot(jnp.where(same, 1.0, 0.0).astype(LOW), halves)
+    along = [unit[k : k + 1, :] for k in range(3)]
+    lengthwise = whole[8:16] * along[0] + whole[16:24] * along[1] + whole[24:32] * along[2]
     place_row = lax.broadcasted_iota(jnp.int32, (8, EDGES), 0)
-    pull = jnp.where(
-        place_row == 0,
-        whole[1],
-        jnp.where(place_row == 1, whole[2], jnp.where(place_row == 2, whole[3], 0.0)),
-    )
-    lengthwise = jnp.sum(pull * direction, axis=0, keepdims=True)
-    change = (pull - direction * lengthwise) * inverse[...] + direction * whole[0]
+    pull = jnp.where(place_row == 2, whole[24:32], 0.0)
+    pull = jnp.where(place_row == 1, whole[16:24], pull)
+    pull = jnp.where(place_row == 0, whole[8:16], pull)
+    change = (pull - unit[...] * lengthwise) * inverse[...] + unit[...] * whole[0:8]
     high, low = split(change)
     d_rel = jnp.concatenate([high.astype(F32), low.astype(F32)], axis=0).astype(LOW)
 
@@ -431,12 +442,13 @@
         w_o1.T,
         w_o2.reshape(1, 16),
     )
+    operands = tuple(pltpu.with_memory_space_constraint(x, pltpu.HBM) for x in operands)
     held = [pltpu.VMEM(x.shape, x.dtype) for x in operands]
     energies, forces = pl.pallas_call(
         functools.partial(kernel, n_dom, n_slab),
         out_shape=(
-            jax.ShapeDtypeStruct((1, ATOMS), F32),
-            jax.ShapeDtypeStruct((3, ATOMS), F32),
+            pltpu.VMEM((1, ATOMS), F32),
+            pltpu.VMEM((3, ATOMS), F32),
         ),
         in_specs=[pl.BlockSpec(memory_space=pltpu.HBM)] * len(operands),
         out_specs=(
@@ -455,12 +467,12 @@
             pltpu.VMEM((HIDDEN, 16), LOW),
             pltpu.VMEM((HIDDEN, HIDDEN), LOW),
             pltpu.VMEM((2 * CHAN, HIDDEN), LOW),
-            pltpu.VMEM((CHAN, CHAN), LOW),
-            pltpu.VMEM((CHAN, CHAN), LOW),
-            pltpu.VMEM((CHAN, 16), LOW),
+            pltpu.VMEM((32, 2 * CHAN), LOW),
+            pltpu.VMEM((2 * CHAN, 32), LOW),
+            pltpu.VMEM((16, ATOMS), F32),
+            pltpu.VMEM((16, 1), F32),
             pltpu.VMEM((CHAN, ATOMS), F32),
-            pltpu.VMEM((CHAN, ATOMS), F32),
-            pltpu.VMEM((CHAN + 32, EDGES), F32),
+            pltpu.VMEM((32, EDGES), F32),
             pltpu.VMEM((CHAN, EDGES), F32),
             pltpu.VMEM((8, EDGES), F32),
             pltpu.VMEM((8, EDGES), F32),
@@ -488,7 +500,7 @@
             pltpu.SemaphoreType.DMA((4, 8)),
         ],
         compiler_params=pltpu.CompilerParams(
-            collective_id=0, has_side_effects=True, vmem_limit_bytes=64 * 1024 * 1024
+            collective_id=0, has_side_effects=True, vmem_limit_bytes=48 * 1024 * 1024
         ),
     )(*operands)
     return energies.reshape(ATOMS), forces

time: 45.6 us -> 43.8 us (0.961)
  Pallas kernels: 42.9 us -> 41.8 us
  local copies, waits for them, and re-layouts: 1.71 us -> 1.09 us
    pallas_call x1, Pallas kernels: 42.9 us -> 41.8 us  [body(): pl.pallas_call(functools.partial(kernel, n_dom, n_slab), out_shape=(pltpu...]
    unnamed x6 -> x2, local copies, waits for them, and re-layouts: 1.71 us -> 1.09 us
where the time goes in v3:
time: 43.8 us; the launch traced here: 43.5 us
  Pallas kernels  41.8 us (95%)
  local copies, waits for them, and re-layouts  1.09 us (2%)
  between operations  0.64 us (1%)
    pallas_call x1, Pallas kernels, body(): pl.pallas_call(functools.partial(kernel, n_dom, n_slab), out_shape=(pltpu...  41.8 us
    unnamed x2, local copies, waits for them, and re-layouts  1.09 us

profile of v3, /device:TPU:6, one launch (start us, length us, event | category | flops | bytes accessed | tf_op | source)
XLA Modules:
  0.0 43.5 jit_solution(12025258407077820374)
XLA Ops:
  0.6 41.8 %shard_map.140 = (f32[1,128]{1,0:T(1,128)S(1)}, f32[3,128]{1,0:T(4,128)S(1)}) custom-call(bf16[128,128]{1,0:T(8,128)(2,1)} %features_hbm.1, f32[3,128]{1,0:T(4,128)} %positions_hbm.1, s32[32,128]{1,0:T(8,128)} %neighbours_hbm.1, s32[32,128]{1,0:T(8,128)} %mask_hbm.1, s32[1,32]{1,0:T(1,128)} %bitcast.6, bf16[128,128]{1,0:T(8,128)(2,1)} %w_up_hbm.1, ...), custom_call_target="tpu_custom_call" | custom-call | tf_op jit(solution)/shard_map/pallas_call | solution.py:447
  42.4 0.5 %copy.17 = f32[128]{0:T(128)} copy(f32[128]{0:T(128)S(1)} %bitcast.4) | data formatting | bytes 1024
  42.9 0.6 %copy.18 = f32[3,128]{1,0:T(4,128)} copy(f32[3,128]{1,0:T(4,128)S(1)} %get-tuple-element.7) | data formatting | bytes 3072

commit v4 on v3

--- a/solution.py
+++ b/solution.py
@@ -353,23 +353,31 @@
 
     for copy in copies3:
         copy.wait_recv()
-    ghost_cot = recv3[...].astype(F32).T.astype(LOW)
-    partner_cot[...] = dot(ghost_cot, hot[ATOMS:ROWS, :])
-    for i in range(SLOTS):
-        tile = tile_of(i)
-        toward = [unit[k : k + 1, tile] for k in range(3)]
-        sums = [partial[8 * k : 8 * k + 8, tile] for k in range(4)]
-        for b in range(BANDS):
-            weight = factors[band(2, b), tile]
-            flow = jnp.zeros((BAND, ATOMS), F32)
+    wide = CHAN // 4
+    ghost_cot = recv3[...].astype(F32).T
+    stacks = [
+        jnp.concatenate(
+            [ghost_cot[k * CHAN + h * wide : k * CHAN + (h + 1) * wide] for k in range(4)], axis=0
+        ).astype(LOW)
+        for h in range(4)
+    ]
+    for c in range(EDGES // 256):
+        lanes = pl.ds(c * 256, 256)
+        toward = [unit[k : k + 1, lanes] for k in range(3)]
+        sums = [partial[8 * k : 8 * k + 8, lanes] for k in range(4)]
+        for h in range(4):
+            far = dot(stacks[h], hot[ATOMS:ROWS, lanes])
+            rows = [pl.ds(k * CHAN + h * wide, wide) for k in range(3)]
+            weight = factors[rows[2], lanes]
+            flow = toward[0] * far[wide : 2 * wide]
+            for k in range(1, 3):
+                flow = flow + toward[k] * far[(k + 1) * wide : (k + 2) * wide]
             for k in range(3):
-                far = partner_cot[band(k + 1, b), tile]
-                flow = flow + toward[k] * far
-                sums[k + 1] = sums[k + 1] - fold(weight * far)
-            spread_part = factors[band(0, b), tile] * partner_cot[band(0, b), tile]
-            sums[0] = sums[0] + fold(spread_part - factors[band(1, b), tile] * flow)
+                sums[k + 1] = sums[k + 1] - fold(weight * far[(k + 1) * wide : (k + 2) * wide])
+            spread_part = factors[rows[0], lanes] * far[0:wide]
+            sums[0] = sums[0] + fold(spread_part - factors[rows[1], lanes] * flow)
         for k in range(4):
-            partial[8 * k : 8 * k + 8, tile] = sums[k]
+            partial[8 * k : 8 * k + 8, lanes] = sums[k]
     high, low = split(partial[...])
     halves = jnp.concatenate([high, low], axis=0)
     row = lax.broadcasted_iota(jnp.int32, (32, 64), 0)

time: 43.8 us -> 43.8 us (level)
  no operation moved by 1% of the time
where the time goes in v4:
time: 43.8 us; the launch traced here: 43.5 us
  Pallas kernels  41.7 us (95%)
  local copies, waits for them, and re-layouts  1.09 us (2%)
  between operations  0.64 us (1%)
    pallas_call x1, Pallas kernels, body(): pl.pallas_call(functools.partial(kernel, n_dom, n_slab), out_shape=(pltpu...  41.7 us
    unnamed x2, local copies, waits for them, and re-layouts  1.09 us

profile of v4, /device:TPU:6, one launch (start us, length us, event | category | flops | bytes accessed | tf_op | source)
XLA Modules:
  0.0 43.5 jit_solution(13154748634964091557)
XLA Ops:
  0.6 41.7 %shard_map.140 = (f32[1,128]{1,0:T(1,128)S(1)}, f32[3,128]{1,0:T(4,128)S(1)}) custom-call(bf16[128,128]{1,0:T(8,128)(2,1)} %features_hbm.1, f32[3,128]{1,0:T(4,128)} %positions_hbm.1, s32[32,128]{1,0:T(8,128)} %neighbours_hbm.1, s32[32,128]{1,0:T(8,128)} %mask_hbm.1, s32[1,32]{1,0:T(1,128)} %bitcast.6, bf16[128,128]{1,0:T(8,128)(2,1)} %w_up_hbm.1, ...), custom_call_target="tpu_custom_call" | custom-call | tf_op jit(solution)/shard_map/pallas_call | solution.py:455
  42.4 0.5 %copy.17 = f32[128]{0:T(128)} copy(f32[128]{0:T(128)S(1)} %bitcast.4) | data formatting | bytes 1024
  42.9 0.6 %copy.18 = f32[3,128]{1,0:T(4,128)} copy(f32[3,128]{1,0:T(4,128)S(1)} %get-tuple-element.7) | data formatting | bytes 3072
